TPU v7x, 32 devices: a whole 2x2x4 slice. The times are simulated.
32 devices in a mesh: row: 8 (over z, y), col: 4 (over x, core).
Axes of the slice: x: 2, y: 2, z: 4, core: 2. Of those that a mesh axis runs over, the one named last changes fastest.
Arguments:
- embedding: bfloat16 [4, 8, 48, 256], P('col', 'row'), may hold values from -0.3984375 to 0.3984375
- preference: float32 [1536], P('row'), may hold values from -2.5 to -0.5
Outputs:
- responsibility: float32 [1536, 1536], P('row', 'col')
- availability: float32 [1536, 1536], P('row', 'col')
All inputs are finite; a program needn't handle non-finite values.
Results may differ from a plain program's by a relative error of at most 0.0003.
Values may be sent and summed in bfloat16 or wider, within the bound.
No kernel may reach another device: no remote copies, remote signals or barrier semaphores. Data moves between devices by JAX's collectives and lax.ppermute only.
A program may use at most 64 MiB of HBM per device.

v0:
```python
import jax
import jax.numpy as jnp
from jax import lax
from jax.sharding import PartitionSpec as P

ITERS = 2


DAMPING = 0.5


def broadcast(block, axis, source):
    block = jnp.where(lax.axis_index(axis) == source, block, jnp.zeros_like(block))
    return lax.psum(block, axis)


def similarity(row_emb, col_emb, row_start, col_start, pref_rows):
    cross = lax.dot_general(
        row_emb, col_emb, (((1,), (1,)), ((), ())), preferred_element_type=jnp.float32
    )
    row_vals = row_emb.astype(jnp.float32)
    col_vals = col_emb.astype(jnp.float32)
    row_sq = jnp.sum(row_vals * row_vals, axis=1)
    col_sq = jnp.sum(col_vals * col_vals, axis=1)
    dist = 2.0 * cross - row_sq[:, None] - col_sq[None, :]
    row_ids = row_start + jnp.arange(row_emb.shape[0], dtype=jnp.int32)
    col_ids = col_start + jnp.arange(col_emb.shape[0], dtype=jnp.int32)
    diagonal = row_ids[:, None] == col_ids[None, :]
    return (jnp.where(diagonal, pref_rows[:, None], dist), diagonal)


def top_two(summed):
    first = jnp.max(summed, axis=1)
    hits = summed == first[:, None]
    repeats = jnp.sum(hits.astype(jnp.int32), axis=1)
    others = jnp.max(jnp.where(hits, -jnp.inf, summed), axis=1)
    second = jnp.where(repeats > 1, first, others)
    return (first, second)


def local(embedding, preference):
    rows_n = lax.axis_size("row")
    cols_n = lax.axis_size("col")
    row_idx = lax.axis_index("row")
    col_idx = lax.axis_index("col")
    mol = embedding.shape[2]
    width = embedding.shape[3]
    row_count = mol * cols_n
    col_count = mol * rows_n
    column_block = lax.all_gather(embedding, "row", axis=1, tiled=True).reshape(col_count, width)
    offset = row_idx * cols_n % rows_n
    root = row_idx * cols_n // rows_n
    own_slice = lax.dynamic_slice_in_dim(column_block, offset * mol, row_count, 0)
    row_block = broadcast(own_slice, "col", root)
    row_start = row_idx * row_count
    col_start = col_idx * col_count
    sim, diagonal = similarity(row_block, column_block, row_start, col_start, preference)
    resp = jnp.zeros_like(sim)
    avail = jnp.zeros_like(sim)
    for step in range(ITERS):
        summed = avail + sim
        local_first, local_second = top_two(summed)
        firsts, seconds = (
            lax.all_gather(local_first, "col", axis=0, tiled=True),
            lax.all_gather(local_second, "col", axis=0, tiled=True),
        )
        firsts = firsts.reshape(cols_n, row_count)
        seconds = seconds.reshape(cols_n, row_count)
        first = jnp.max(firsts, axis=0)
        at_top = firsts == first[None, :]
        repeats = jnp.sum(at_top.astype(jnp.int32), axis=0)
        others = jnp.max(jnp.where(at_top, -jnp.inf, firsts), axis=0)
        second = jnp.where(repeats > 1, first, jnp.maximum(jnp.max(seconds, axis=0), others))
        fresh = sim - jnp.where(summed == first[:, None], second[:, None], first[:, None])
        resp = DAMPING * resp + (1.0 - DAMPING) * fresh
        positive = jnp.where(diagonal, resp, jnp.maximum(resp, 0.0))
        colsum = lax.psum(jnp.sum(positive, axis=0), "row")
        renew = colsum[None, :] - positive
        renew = jnp.where(diagonal, renew, jnp.minimum(renew, 0.0))
        avail = DAMPING * avail + (1.0 - DAMPING) * renew
    return (resp, avail)


def solution(mesh):
    placed = (P("col", "row", None, None), P("row"))
    return jax.shard_map(
        local,
        mesh=mesh,
        in_specs=placed,
        out_specs=(P("row", "col"), P("row", "col")),
        check_vma=False,
    )
```

profile of v0, /device:TPU:0, one launch (start us, length us, event | category | flops | bytes accessed | tf_op | source)
XLA Modules:
  0.0 135.7 jit_solution(3595464313842776893)
XLA Ops:
  7.2 0.0 all-reduce.8.cloned.1.call-start
  7.2 0.0 copy-start.2
  7.2 0.7 copy-done.2
  8.0 32.4 %all_gather.15 = bf16[1,8,48,256]{3,2,0,1:T(8,128)(2,1)S(1)} all-gather(bf16[1,1,48,256]{3,2,0,1:T(8,128)(2,1)S(1)} %bitcast.7), channel_id=1, replica_groups=mesh['row'=8,'col'=4] {'row'}, dimensions={1}, use_global_device_ids=true | all-gather | bytes 221184 | tf_op jit(solution)/shard_map/all_gather | solution.py:50
  40.4 0.7 dynamic-slice_select_fusion
  41.0 0.0 all-reduce.8.cloned.1.call-update
  41.0 0.1 multiply_reduce_fusion
  41.2 0.0 copy-start.4
  41.2 0.1 sub.47
  41.3 0.6 copy-done.4
  41.9 0.6 dynamic-slice
  43.1 0.0 copy-start.3
  43.1 30.3 %all-reduce.8.cloned.1.call-done = bf16[192,256]{1,0:T(8,128)(2,1)} async-done(((bf16[192,256]{1,0:T(8,128)(2,1)}), bf16[192,256]{1,0:T(8,128)(2,1)}) %all-reduce.8.cloned.1.call-update) | async-done | bytes 98320 | tf_op jit(solution)/shard_map/psum | solution.py:14
  73.5 0.0 copy-start.1
  73.5 1.1 multiply_reduce_fusion.1
  74.5 0.0 copy-done.3
  74.5 0.0 copy-done.1
  74.6 0.3 fusion.18
  74.9 0.2 fusion.4
  75.1 0.2 fusion.3
  75.3 0.2 dynamic-update-slice
  75.5 0.1 fusion.15
  75.6 5.8 %all-reduce.5 = (f32[768]{0:T(1024)S(1)}, f32[768]{0:T(1024)S(1)}) all-reduce(f32[768]{0:T(1024)S(1)} %dynamic-update-slice, f32[768]{0:T(1024)S(1)} %fusion.15), channel_id=1, replica_groups=mesh['row'=8,'col'=4] {'col'}, use_global_device_ids=true, to_apply=%add | all-reduce | flops 1536 | bytes 12288
  81.5 0.1 reshape.63
  81.6 0.1 reshape.64
  81.7 0.2 fusion.10
  81.9 21.5 %psum.22 = f32[384]{0:T(512)S(1)} all-reduce(f32[384]{0:T(512)S(1)} %fusion.10), channel_id=1, replica_groups=mesh['row'=8,'col'=4] {'row'}, use_global_device_ids=true, to_apply=%region_11.12 | all-reduce | flops 384 | bytes 3072 | tf_op jit(solution)/shard_map/psum | solution.py:77
  103.4 0.3 fusion.17
  103.7 0.2 fusion.5
  103.9 0.2 fusion.6
  104.1 0.2 dynamic-update-slice.2
  104.3 0.1 fusion.16
  104.4 5.8 %all-reduce.4 = (f32[768]{0:T(1024)S(1)}, f32[768]{0:T(1024)S(1)}) all-reduce(f32[768]{0:T(1024)S(1)} %dynamic-update-slice.2, f32[768]{0:T(1024)S(1)} %fusion.16), channel_id=1, replica_groups=mesh['row'=8,'col'=4] {'col'}, use_global_device_ids=true, to_apply=%add.2 | all-reduce | flops 1536 | bytes 12288
  110.3 0.1 reshape.65
  110.4 0.1 reshape.66
  110.5 0.2 fusion.9
  110.7 0.0 copy-start
  110.7 17.1 %psum.23 = f32[384]{0:T(512)S(1)} all-reduce(f32[384]{0:T(512)S(1)} %get-tuple-element.6), channel_id=1, replica_groups=mesh['row'=8,'col'=4] {'row'}, use_global_device_ids=true, to_apply=%region_20.21 | all-reduce | flops 384 | bytes 3072 | tf_op jit(solution)/shard_map/psum | solution.py:77
  127.9 1.0 fusion.8
  128.8 0.0 copy-done
  (16 shorter events, 0.2 us)
Async XLA Ops:
  7.2 66.3 %all-reduce.8.cloned.1.call-start = ((), (), s32[]{:S(2)}) async-start(), calls=%async_computation | async-start | bytes 196608 | tf_op jit(solution)/shard_map/psum | solution.py:14
  7.2 0.7 copy-start.2
  41.2 0.7 copy-start.4
  43.1 31.4 %copy-start.3 = (f32[192]{0:T(256)S(1)}, f32[192]{0:T(256)}, u32[]{:S(2)}) copy-start(f32[192]{0:T(256)} %param.3) | copy-start | bytes 2308
  73.5 1.1 copy-start.1
  110.7 18.1 %copy-start = (f32[192,384]{1,0:T(8,128)}, f32[192,384]{1,0:T(8,128)S(1)}, u32[]{:S(2)}) copy-start(f32[192,384]{1,0:T(8,128)S(1)} %get-tuple-element.7) | copy-start | bytes 884740
Sparse Core Ops, SparseCore 0:
  41.2 32.2 all-reduce.7
where the time goes:
time: 136 us
  blocking collectives  82.7 us (61%)
  waiting for transfers between devices  30.4 us (22%)
  between operations  14.9 us (11%)
  other arithmetic  4.63 us (3%)
  local copies, waits for them, and re-layouts  2.77 us (2%)
    psum x2, blocking collectives, local(): colsum = lax.psum(jnp.sum(positive, axis=0), 'row')  38.6 us
    all_gather x1, blocking collectives, local(): lax.all_gather(embedding, 'row', axis=1, tiled=True)  32.4 us
    psum x1, waiting for transfers between devices, broadcast(): return lax.psum(block, axis)  30.3 us
    unnamed x2, blocking collectives  11.7 us
  transfers between devices with their start and end apart: 1, of which 1 were waited for; matrix products, arithmetic and copies ran while one was open for 1% of the time, Pallas kernels for 0%

commit v1 on v0

--- a/solution.py
+++ b/solution.py
@@ -1,12 +1,181 @@
+import functools
+import math
+
 import jax
 import jax.numpy as jnp
 from jax import lax
+from jax.experimental import pallas as pl
+from jax.experimental.pallas import tpu as pltpu
 from jax.sharding import PartitionSpec as P
 
 ITERS = 2
-
-
 DAMPING = 0.5
+LOW = -1e30
+
+
+def push(one, two, item):
+    return jnp.maximum(one, item), jnp.maximum(two, jnp.minimum(one, item))
+
+def fold(one, two):
+    for shift in (4, 2, 1):
+        o, t = pltpu.roll(one, shift, 0), pltpu.roll(two, shift, 0)
+        one, two = jnp.maximum(one, o), jnp.maximum(jnp.minimum(one, o), jnp.maximum(two, t))
+    return one, two
+
+def kernel(rows, cols, win, x_ref, pref_ref, at_ref, resp_ref, avail_ref, g_ref, c_ref, q_ref, row_ref, r_out, a_out, T=256, CH=16, L4=16):
+    n, width = x_ref.shape
+    def qbody(j, _):
+        s = pl.ds(pl.multiple_of(j * 64, 64), 64)
+        x = x_ref[s, :].astype(jnp.float32)
+        q_ref[s, :] = jnp.broadcast_to(jnp.sum(x * x, axis=1, keepdims=True), (64, 128))
+        return 0
+    lax.fori_loop(0, n // 64, qbody, 0)
+    eye = lax.broadcasted_iota(jnp.int32, (T, T), 0) == lax.broadcasted_iota(jnp.int32, (T, T), 1)
+    for t in range(n // T):
+        lanes = slice(t * T, (t + 1) * T)
+        xt = x_ref[lanes, :] * jnp.bfloat16(2)
+        def product(start):
+            s = pl.ds(start, T)
+            p = lax.dot_general(x_ref[s, :], xt, (((1,), (1,)), ((), ())), preferred_element_type=jnp.float32)
+            qq = q_ref[s, :]
+            return p, p - jnp.concatenate([qq] * (T // 128), axis=1)
+        def take(g, m):
+            one, two = m
+            for r in range(0, T, 8):
+                one, two = push(one, two, g[r:r + 8, :])
+            return one, two
+        p, g = product(t * T)
+        dq = jnp.sum(jnp.where(eye, p, 0.0), axis=0, keepdims=True)
+        own = pref_ref[:, lanes] + 0.5 * dq
+        g = jnp.where(eye, LOW, g)
+        g_ref[lanes, lanes] = g
+        m = (jnp.full((8, T), LOW), jnp.full((8, T), LOW))
+        m = take(g, m)
+        def body(j, m):
+            b = j + (j >= t).astype(jnp.int32)
+            st = pl.multiple_of(b * T, T)
+            p, g = product(st)
+            g_ref[pl.ds(st, T), lanes] = g
+            return take(g, m)
+        m = lax.fori_loop(0, n // T - 1, body, m)
+        one, two = fold(*m)
+        own = jnp.broadcast_to(own, (8, T))
+        one, two = push(one, two, own)
+        row_ref[0, :, lanes] = one
+        row_ref[1, :, lanes] = 0.25 * (one - two)
+        row_ref[2, :, lanes] = own
+        row_ref[3, :, lanes] = 0.5 * (own - jnp.where(own == one, two, one))
+        row_ref[4, :, lanes] = jnp.zeros((8, T), jnp.float32)
+    sub = lax.broadcasted_iota(jnp.int32, (CH, 128), 0)
+    lane = lax.broadcasted_iota(jnp.int32, (CH, 128), 1)
+    first = row_ref[0]; gain = row_ref[1]
+    def body(j, m):
+        one, two = m
+        st = pl.multiple_of(j * CH, CH)
+        s = pl.ds(st, CH)
+        lb = pl.ds(pl.multiple_of((j * CH // 128) * 128, 128), 128)
+        d = lane - sub == lax.rem(j * CH, 128)
+        g = g_ref[s, :]
+        w = jnp.concatenate([jnp.where(g[r:r+8] == first, gain, 0.0) for r in range(0, CH, 8)], 0)
+        acc = w[:, 0:128]
+        for l in range(128, n, 128):
+            acc = acc + w[:, l:l + 128]
+        diag = jnp.concatenate([row_ref[3, :, lb]] * (CH // 8), 0)
+        acc = acc + jnp.where(d, 0.5 * diag, 0.0)
+        c = jnp.broadcast_to(jnp.sum(acc, axis=1, keepdims=True), (CH, 128))
+        c_ref[s, :] = c
+        dd = jnp.where(d, c, 0.0)
+        tot = dd[0:8]
+        for r in range(8, CH, 8): tot = tot + dd[r:r+8]
+        row_ref[4, :, lb] += tot
+        u = g + jnp.minimum(jnp.concatenate([c] * (n // 128), 1) - w, 0.0)
+        for r in range(0, CH, 8):
+            one, two = push(one, two, u[r:r + 8])
+        return one, two
+    m = lax.fori_loop(0, n // CH, body, (jnp.full((8, n), LOW), jnp.full((8, n), LOW)))
+    one, two = fold(*m)
+    half = jnp.sum(row_ref[4], axis=0, keepdims=True)
+    own = row_ref[2]; r1d = row_ref[3]
+    av1d = jnp.broadcast_to(half, (8, n)) - 0.5 * r1d
+    own2 = own + av1d
+    one, two = push(one, two, own2)
+    base = 0.25 * first + 0.5 * one
+    z = 0.5 * (one - two)
+    r2d = 0.5 * r1d + 0.5 * (own - jnp.where(own2 == one, two, one))
+    row_ref[4] = one
+    row_ref[5] = base
+    row_ref[6] = z
+    row_ref[7] = r2d
+    row_ref[8] = av1d
+    r0 = at_ref[0]; c0 = at_ref[1]
+    sub4 = lax.broadcasted_iota(jnp.int32, (L4, 128), 0)
+    lane4 = lax.broadcasted_iota(jnp.int32, (L4, 128), 1)
+    tile = lambda a, k: jnp.concatenate([a] * k, 0)
+    def resp2(g, c, first, gain, one, base, z):
+        w = jnp.where(g == first, gain, 0.0)
+        t = jnp.minimum(c - w, 0.0)
+        return (0.75 * g - base) + (w + jnp.where(g + t == one, z, 0.0)), t
+    w0 = pl.multiple_of((r0 // 128) * 128, 128)
+    def body4(j, _):
+        st = pl.multiple_of(c0 + j * L4, L4)
+        s = pl.ds(st, L4)
+        lb = pl.ds(pl.multiple_of((st // 128) * 128, 128), 128)
+        d = lane4 - sub4 == lax.rem(st, 128)
+        c = c_ref[s, :]
+        acc = jnp.where(d, tile(row_ref[7, :, lb], L4 // 8), 0.0)
+        for l in range(0, n, 128):
+            k = slice(l, l + 128)
+            f = lambda i: tile(row_ref[i, :, k], L4 // 8)
+            r2, _ = resp2(g_ref[s, k], c, f(0), f(1), f(4), f(5), f(6))
+            acc = acc + jnp.maximum(r2, 0.0)
+        cs = 0.5 * jnp.broadcast_to(jnp.sum(acc, axis=1, keepdims=True), (L4, 128))
+        for l in range(0, win, 128):
+            lw = pl.ds(w0 + l, 128)
+            f = lambda i: tile(row_ref[i, :, lw], L4 // 8)
+            r2, t = resp2(g_ref[s, lw], c, f(0), f(1), f(4), f(5), f(6))
+            a2 = 0.5 * t + jnp.minimum(cs - 0.5 * jnp.maximum(r2, 0.0), 0.0)
+            dg = lane4 + (w0 + l) == sub4 + st
+            rd = f(7)
+            r2 = jnp.where(dg, rd, r2)
+            a2 = jnp.where(dg, 0.5 * f(8) + (cs - 0.5 * rd), a2)
+            o = pl.ds(pl.multiple_of(j * L4, L4), L4)
+            r_out[o, l:l + 128] = r2
+            a_out[o, l:l + 128] = a2
+        return 0
+    lax.fori_loop(0, cols // L4, body4, 0)
+    off = pl.multiple_of(r0 - w0, 8)
+    g_ref[0:win, 0:cols] = r_out[...].T
+    g_ref[win:2 * win, 0:cols] = a_out[...].T
+    resp_ref[...] = g_ref[pl.ds(off, rows), 0:cols]
+    avail_ref[...] = g_ref[pl.ds(win + off, rows), 0:cols]
+
+def compute(x, pref, at, rows, cols, **kw):
+    n = x.shape[0]
+    win = -(-(rows + 128 - math.gcd(rows, 128)) // 128) * 128
+    f32 = jnp.float32
+    return pl.pallas_call(
+        functools.partial(kernel, rows, cols, win, **kw),
+        out_shape=[jax.ShapeDtypeStruct((rows, cols), f32)] * 2,
+        in_specs=[pl.BlockSpec(memory_space=pltpu.VMEM)] * 2 + [pl.BlockSpec(memory_space=pltpu.SMEM)],
+        out_specs=[pl.BlockSpec(memory_space=pltpu.VMEM)] * 2,
+        scratch_shapes=[pltpu.VMEM((n, n), f32), pltpu.VMEM((n, 128), f32), pltpu.VMEM((n, 128), f32), pltpu.VMEM((9, 8, n), f32),
+                        pltpu.VMEM((cols, win), f32), pltpu.VMEM((cols, win), f32)],
+        compiler_params=pltpu.CompilerParams(vmem_limit_bytes=48 << 20),
+    )(x, pref, at)
+
+
+def local(embedding, preference):
+    rows_n, cols_n = lax.axis_size("row"), lax.axis_size("col")
+    mol, width = embedding.shape[2:]
+    total = mol * rows_n * cols_n
+    rows, cols = mol * cols_n, mol * rows_n
+    if 4 * total * total > 24 << 20:
+        return tiled(embedding, preference)
+    part = lax.all_gather(embedding.reshape(mol, width), "row", axis=0, tiled=True)
+    x = lax.all_gather(part, "col", axis=0, tiled=True)
+    pref = lax.all_gather(preference, "row", axis=0, tiled=True).reshape(1, total)
+    at = jnp.stack([lax.axis_index("row") * rows, lax.axis_index("col") * cols]).astype(jnp.int32)
+    return tuple(compute(x, pref, at, rows, cols))
 
 
 def broadcast(block, axis, source):
@@ -38,7 +207,7 @@
     return (first, second)
 
 
-def local(embedding, preference):
+def tiled(embedding, preference):
     rows_n = lax.axis_size("row")
     cols_n = lax.axis_size("col")
     row_idx = lax.axis_index("row")

time: 136 us -> 92.9 us (0.68)
  waiting for transfers between devices: 30.4 us -> 0 us
  Pallas kernels: 0 us -> 27.3 us
  blocking collectives: 82.7 us -> 62.5 us
  between operations: 14.9 us -> 1.36 us
  other arithmetic: 4.63 us -> 0.08 us
    psum x2 -> x0, blocking collectives: 38.6 us -> none  [local(): colsum = lax.psum(jnp.sum(positive, axis=0), 'row')]
    psum x1 -> x0, waiting for transfers between devices: 30.3 us -> none  [broadcast(): return lax.psum(block, axis)]
    pallas_call x0 -> x1, Pallas kernels: none -> 27.3 us  [compute(): pl.pallas_call(functools.partial(kernel, rows, cols, win, **kw), out_shap...]
    unnamed x2 -> x1, blocking collectives: 11.7 us -> 23.3 us
    all_gather x1 -> x2, blocking collectives: 32.4 us -> 39.2 us  [the longest x1 30.6 us: local(): lax.all_gather(embedding.reshape(mol, width), 'row', axis=0, tiled=True)]
    reduce_sum x8 -> x0, other arithmetic: 1.99 us -> none  [the longest x1 1.08 us: similarity(): row_sq = jnp.sum(row_vals * row_vals, axis=1)]
  transfers between devices with their start and end apart: 1 -> 0, of which waited for: 1 -> 0; matrix products, arithmetic and copies ran while one was open for 1% -> 0% of each run, Pallas kernels for 0% -> 0%
where the time goes in v1:
time: 92.9 us; the launch traced here: 92.7 us
  blocking collectives  62.5 us (67%)
  Pallas kernels  27.3 us (29%)
  local copies, waits for them, and re-layouts  1.44 us (2%)
  between operations  1.36 us (1%)
    all_gather x1, blocking collectives, local(): lax.all_gather(embedding.reshape(mol, width), 'row', axis=0, tiled=True)  30.6 us
    pallas_call x1, Pallas kernels, compute(): pl.pallas_call(functools.partial(kernel, rows, cols, win, **kw), out_shap...  27.3 us
    unnamed x1, blocking collectives  23.3 us
    all_gather x1, blocking collectives, local(): x = lax.all_gather(part, 'col', axis=0, tiled=True)  8.58 us

profile of v1, /device:TPU:0, one launch (start us, length us, event | category | flops | bytes accessed | tf_op | source)
XLA Modules:
  0.0 92.7 jit_solution(5948449682291278945)
XLA Ops:
  0.6 0.0 copy-start.2
  0.6 0.0 copy-start.1
  0.7 0.0 copy-start
  0.7 0.1 pad_add_fusion.at_ref
  0.7 0.6 copy-done.2
  1.3 0.6 dynamic-slice
  2.5 0.0 copy-done.1
  2.6 0.3 dynamic-update-slice
  2.8 23.3 %all-reduce = f32[1536]{0:T(1024)S(1)} all-reduce(f32[1536]{0:T(1024)S(1)} %dynamic-update-slice), channel_id=1, replica_groups=mesh['row'=8,'col'=4] {'row'}, use_global_device_ids=true, to_apply=%add | all-reduce | flops 1536 | bytes 12288
  26.2 0.0 copy-done
  26.2 30.6 %all-gather = bf16[1,1,384,256]{3,2,1,0:T(8,128)(2,1)S(1)} all-gather(bf16[1,1,48,256]{3,2,1,0:T(8,128)(2,1)S(1)} %copy-done), channel_id=2, replica_groups=mesh['row'=8,'col'=4] {'row'}, dimensions={2}, use_global_device_ids=true | all-gather | bytes 221184 | tf_op jit(solution)/shard_map/all_gather | solution.py:174
  56.8 8.6 %all-gather.1 = bf16[1,1,1536,256]{3,2,1,0:T(8,128)(2,1)S(1)} all-gather(bf16[1,1,384,256]{3,2,1,0:T(8,128)(2,1)S(1)} %all-gather), channel_id=3, replica_groups=mesh['row'=8,'col'=4] {'col'}, dimensions={2}, use_global_device_ids=true | all-gather | bytes 983040 | tf_op jit(solution)/shard_map/all_gather | solution.py:175
  65.4 27.3 %shard_map.41 = (f32[192,384]{1,0:T(8,128)}, f32[192,384]{1,0:T(8,128)}) custom-call(bf16[1536,256]{1,0:T(8,128)(2,1)S(1)} %bitcast.4, f32[1,1536]{1,0:T(1,128)S(1)} %reshape.11.pref_ref, s32[2]{0:T(128)S(1)} %pad_add_fusion.at_ref), custom_call_target="tpu_custom_call" | custom-call | tf_op jit(solution)/shard_map/pallas_call | solution.py:156
  (2 shorter events, 0.0 us)
Async XLA Ops:
  0.6 0.7 copy-start.2
  0.6 1.9 %copy-start.1 = (f32[192]{0:T(256)S(1)}, f32[192]{0:T(256)}, u32[]{:S(2)}) copy-start(f32[192]{0:T(256)} %param.3) | copy-start | bytes 2308
  0.7 25.5 %copy-start = (bf16[1,1,48,256]{3,2,1,0:T(8,128)(2,1)S(1)}, bf16[1,1,48,256]{3,2,1,0:T(8,128)(2,1)}, u32[]{:S(2)}) copy-start(bf16[1,1,48,256]{3,2,1,0:T(8,128)(2,1)} %param.2) | copy-start | bytes 73732

commit v2 on v0

--- a/solution.py
+++ b/solution.py
@@ -1,12 +1,288 @@
+import functools
+import math
+
 import jax
 import jax.numpy as jnp
 from jax import lax
+from jax.experimental import pallas as pl
+from jax.experimental.pallas import tpu as pltpu
 from jax.sharding import PartitionSpec as P
 
 ITERS = 2
-
-
 DAMPING = 0.5
+LOW = -1e30
+LANES = 128
+NT = (((1,), (1,)), ((), ()))
+F32, BF16 = jnp.float32, jnp.bfloat16
+
+
+def push(one, two, item):
+    return jnp.maximum(one, item), jnp.maximum(two, jnp.minimum(one, item))
+
+
+def merge(one, two, o, t):
+    return jnp.maximum(one, o), jnp.maximum(jnp.minimum(one, o), jnp.maximum(two, t))
+
+
+def fold(one, two, at=None):
+    for shift in (4, 2, 1):
+        o, t = pltpu.roll(one, shift, 0), pltpu.roll(two, shift, 0)
+        if at is not None:
+            a = pltpu.roll(at, shift, 0)
+            at = jnp.where((o > one) | ((o == one) & (a < at)), a, at)
+        one, two = merge(one, two, o, t)
+    return one, two, at
+
+
+def thirds(value):
+    high = value.astype(BF16).astype(F32)
+    rest = value - high
+    mid = rest.astype(BF16).astype(F32)
+    return high, mid, rest - mid
+
+
+def squares(x_ref, q_ref, step):
+    n, width = x_ref.shape
+    ones = jnp.ones((2 * width, LANES), BF16)
+    for s in range(0, n, step):
+        x = x_ref[s:s + step, :].astype(F32)
+        x = x * x
+        high = x.astype(BF16)
+        low = (x - high.astype(F32)).astype(BF16)
+        q_ref[s:s + step, :] = jnp.dot(jnp.concatenate([high, low], 1), ones, preferred_element_type=F32)
+
+
+def unpack(mesh_n, mol, masks, me, halves, x_ref, pref_ref):
+    rows_n, cols_n = mesh_n
+    seen = set()
+    for half, flip in zip(halves, (0, 1)):
+        for p, mask in enumerate(masks):
+            owner = me ^ (mask ^ flip)
+            row, col = owner // cols_n, owner % cols_n
+            at = p * (mol + 8)
+            x_ref[pl.ds(pl.multiple_of((col * rows_n + row) * mol, 16), mol), :] = half[at:at + mol, :]
+            if (mask ^ flip) // cols_n not in seen:
+                seen.add((mask ^ flip) // cols_n)
+                tail = half[at + mol:at + mol + 8, :].astype(F32)
+                pref_ref[pl.ds(row, 1), :] = (tail[0:1] + tail[1:2]) + tail[2:3]
+
+
+FIRST, GAIN, OWN, R1D, ONE, TWO, BASE, Z, R2D, AV1D, STAR, WZ = range(12)
+
+
+def kernel(mesh_n, mol, masks, rows, cols, win, sent_ref, came_ref, resp_ref, avail_ref, x_ref, pref_ref, g_ref, c_ref, q_ref, row_ref, k_ref, r_out, a_out,
+           T=512, R=256, CH=128, QS=256):
+    n, width = x_ref.shape
+    rows_n, cols_n = mesh_n
+    row_idx, col_idx = lax.axis_index("row"), lax.axis_index("col")
+    unpack(mesh_n, mol, masks, row_idx * cols_n + col_idx, (sent_ref, came_ref), x_ref, pref_ref)
+    squares(x_ref, q_ref, QS)
+    sub8 = lax.broadcasted_iota(jnp.int32, (8, LANES), 0)
+    lane8 = lax.broadcasted_iota(jnp.int32, (8, LANES), 1)
+    gap = lane8 - sub8
+    pref = jnp.concatenate([pref_ref[r:r + 1, 0:rows] for r in range(rows_n)], 1)
+    blocks = n // LANES
+    low8 = jnp.full((8, LANES), LOW, F32)
+    for t in range(0, n, T):
+        xt = x_ref[t:t + T, :] * BF16(2)
+        K = T // LANES
+        one, two, at = [low8] * K, [low8] * K, [jnp.zeros((8, LANES), jnp.int32)] * K
+        dq = [jnp.zeros((8, LANES), F32)] * K
+        for b in range(0, n, R):
+            p = lax.dot_general(x_ref[b:b + R, :], xt, NT, preferred_element_type=F32)
+            for r in range(0, R, 8):
+                q = q_ref[b + r:b + r + 8, :]
+                for l in range(K):
+                    item = p[r:r + 8, l * LANES:(l + 1) * LANES]
+                    lo = t + l * LANES
+                    on = lo <= b + r < lo + LANES
+                    if on:
+                        mask = gap == b + r - lo
+                        dq[l] = dq[l] + jnp.where(mask, item, 0.0)
+                    item = item - q
+                    if on:
+                        item = jnp.where(mask, LOW, item)
+                    g_ref[b + r:b + r + 8, lo:lo + LANES] = item
+                    at[l] = jnp.where(item > one[l], b + r, at[l])
+                    one[l], two[l] = push(one[l], two[l], item)
+        for l in range(K):
+            lanes = slice(t + l * LANES, t + (l + 1) * LANES)
+            top, next_, a = fold(one[l], two[l], at[l] + sub8)
+            own = jnp.broadcast_to(pref[:, lanes] + 0.5 * jnp.sum(dq[l], axis=0, keepdims=True), (8, LANES))
+            first, second = push(top, next_, own)
+            row_ref[STAR, :, lanes] = top
+            row_ref[FIRST, :, lanes] = first
+            row_ref[GAIN, :, lanes] = jnp.maximum(0.25 * (top - jnp.maximum(next_, own)), 0.0)
+            row_ref[OWN, :, lanes] = own
+            row_ref[R1D, :, lanes] = 0.5 * (own - jnp.where(own == first, second, first))
+            k_ref[0, :, lanes] = a
+            k_ref[1, :, lanes] = a - sub8
+            row_ref[ONE, :, lanes] = low8
+            row_ref[TWO, :, lanes] = low8
+    H = -(-blocks // 16) * 16
+    subL = lax.broadcasted_iota(jnp.int32, (LANES, LANES), 0)
+    subH = lax.broadcasted_iota(jnp.int32, (H, LANES), 0)
+    short, tall = [[], [], []], []
+    for l in range(blocks):
+        lanes = slice(l * LANES, (l + 1) * LANES)
+        k = k_ref[0, 0:1, lanes]
+        tall.append(jnp.where(subL == k % LANES, 1.0, 0.0).astype(BF16))
+        for i, part in enumerate(thirds(row_ref[GAIN, 0:1, lanes])):
+            short[i].append(jnp.where(subH == k // LANES, part, 0.0).astype(BF16))
+    tall = jnp.concatenate(tall, 1)
+    short = jnp.concatenate([jnp.concatenate(s, 1) for s in short], 0)
+    s = lax.dot_general(short, tall, NT, preferred_element_type=F32)
+    s = (s[0:H] + s[H:2 * H]) + s[2 * H:]
+    half = []
+    for l in range(blocks):
+        lanes = slice(l * LANES, (l + 1) * LANES)
+        av = s[l:l + 1, :]
+        row_ref[AV1D, :, lanes] = jnp.broadcast_to(av, (8, LANES))
+        half.append(av + 0.5 * row_ref[R1D, 0:1, lanes])
+    half = jnp.concatenate(half + [jnp.zeros((H - blocks, LANES), F32)] * (H > blocks), 0)
+    half = jnp.concatenate(thirds(half), 0)
+    got = jnp.dot(half.astype(BF16), tall, preferred_element_type=F32)
+    got = (got[0:H] + got[H:2 * H]) + got[2 * H:]
+    pick = lax.broadcasted_iota(jnp.int32, (3 * H, n), 0) % H == lax.broadcasted_iota(jnp.int32, (3 * H, n), 1) // LANES
+    side = jnp.concatenate([half, jnp.zeros((LANES - 3 * H, LANES), F32)], 0).T[:, 0:3 * H].astype(BF16)
+    c_ref[...] = jnp.dot(side, jnp.where(pick, 1.0, 0.0).astype(BF16), preferred_element_type=F32)
+    for l in range(blocks):
+        lanes = slice(l * LANES, (l + 1) * LANES)
+        k = k_ref[0, 0:1, lanes]
+        c = jnp.sum(jnp.where(subH == k // LANES, got[:, lanes], 0.0), axis=0, keepdims=True)
+        row_ref[WZ, :, lanes] = jnp.broadcast_to(c, (8, LANES))
+    def tops(j, _):
+        groups = CH // 8
+        a = [jnp.minimum(c_ref[8 * r:8 * r + 8, pl.ds(pl.multiple_of(j * LANES, LANES), LANES)], 0.0) for r in range(groups)]
+        at = [pl.ds(pl.multiple_of(j * CH + 8 * r, 8), 8) for r in range(groups)]
+        for l in range(blocks):
+            k = slice(l * LANES, (l + 1) * LANES)
+            star = k_ref[1, :, k] - j * CH
+            one, two = row_ref[ONE, :, k], row_ref[TWO, :, k]
+            for r in range(groups):
+                one, two = push(one, two, jnp.where(star == 8 * r, LOW, g_ref[at[r], k] + a[r]))
+            row_ref[ONE, :, k] = one
+            row_ref[TWO, :, k] = two
+        return 0
+    lax.fori_loop(0, n // CH, tops, 0)
+    for l in range(blocks):
+        k = slice(l * LANES, (l + 1) * LANES)
+        one, two, _ = fold(row_ref[ONE, :, k], row_ref[TWO, :, k])
+        own, r1d, first, gain, av1d = (row_ref[i, :, k] for i in (OWN, R1D, FIRST, GAIN, AV1D))
+        t = jnp.minimum(row_ref[WZ, :, k] - gain, 0.0)
+        star = row_ref[STAR, :, k] + t
+        own2 = own + av1d
+        one, two = push(one, two, star)
+        one, two = push(one, two, own2)
+        z = (2 / 3) * (one - two)
+        row_ref[ONE, :, k] = one
+        row_ref[BASE, :, k] = (first + 2.0 * one) * (1 / 3)
+        row_ref[Z, :, k] = z
+        row_ref[R2D, :, k] = 0.5 * r1d + 0.5 * (own - jnp.where(own2 == one, two, one))
+        row_ref[WZ, :, k] = (4 / 3) * gain + jnp.where(star == one, z, 0.0)
+        row_ref[STAR, :, k] = t
+    r0, c0 = row_idx * rows, col_idx * cols
+    w0 = pl.multiple_of((r0 // LANES) * LANES, LANES)
+    def body4(j, _):
+        st = pl.multiple_of(c0 + j * LANES, LANES)
+        groups = LANES // 8
+        at = [pl.ds(pl.multiple_of(st + 8 * r, 8), 8) for r in range(groups)]
+        out = [pl.ds(pl.multiple_of(j * LANES + 8 * r, 8), 8) for r in range(groups)]
+        c = [c_ref[8 * r:8 * r + 8, pl.ds(st, LANES)] for r in range(groups)]
+        a = [jnp.minimum(v, 0.0) for v in c]
+        r2d = (4 / 3) * row_ref[R2D, :, pl.ds(st, LANES)]
+        acc = [jnp.where(gap == 8 * r, r2d, 0.0) for r in range(groups)]
+        def resp2(r, k, star, row):
+            g = g_ref[at[r], k]
+            more = jnp.where(g + a[r] == row[0], row[2], 0.0)
+            return (g - row[1]) + jnp.where(star == 8 * r, row[3], more)
+        for l in range(blocks):
+            k = slice(l * LANES, (l + 1) * LANES)
+            star = k_ref[1, :, k] - st
+            row = [row_ref[i, :, k] for i in (ONE, BASE, Z, WZ)]
+            for r in range(groups):
+                acc[r] = acc[r] + jnp.maximum(resp2(r, k, star, row), 0.0)
+        cs = [0.375 * jnp.broadcast_to(jnp.sum(v, axis=1, keepdims=True), (8, LANES)) for v in acc]
+        for l in range(0, win, LANES):
+            k = pl.ds(pl.multiple_of(w0 + l, LANES), LANES)
+            star = k_ref[1, :, k] - st
+            row = [row_ref[i, :, k] for i in (ONE, BASE, Z, WZ)]
+            rd, ad, ts = row_ref[R2D, :, k], row_ref[AV1D, :, k], row_ref[STAR, :, k]
+            for r in range(groups):
+                r2 = 0.75 * resp2(r, k, star, row)
+                t = jnp.where(star == 8 * r, ts, a[r])
+                a2 = 0.5 * t + jnp.minimum(cs[r] - 0.5 * jnp.maximum(r2, 0.0), 0.0)
+                dg = gap == st + 8 * r - (w0 + l)
+                r_out[out[r], l:l + LANES] = jnp.where(dg, rd, r2)
+                a_out[out[r], l:l + LANES] = jnp.where(dg, 0.5 * ad + (cs[r] - 0.5 * rd), a2)
+        return 0
+    lax.fori_loop(0, cols // LANES, body4, 0)
+    off = pl.multiple_of(r0 - w0, 8)
+    g_ref[0:win, 0:cols] = r_out[...].T
+    g_ref[win:2 * win, 0:cols] = a_out[...].T
+    resp_ref[...] = g_ref[pl.ds(off, rows), 0:cols]
+    avail_ref[...] = g_ref[pl.ds(win + off, rows), 0:cols]
+
+
+def compute(sent, came, mesh_n, mol, masks, rows, cols):
+    n, width = mol * mesh_n[0] * mesh_n[1], sent.shape[1]
+    win = -(-(rows + LANES - math.gcd(rows, LANES)) // LANES) * LANES
+    return pl.pallas_call(
+        functools.partial(kernel, mesh_n, mol, masks, rows, cols, win),
+        out_shape=[jax.ShapeDtypeStruct((rows, cols), F32)] * 2,
+        in_specs=[pl.BlockSpec(memory_space=pltpu.VMEM)] * 2,
+        out_specs=[pl.BlockSpec(memory_space=pltpu.VMEM)] * 2,
+        scratch_shapes=[
+            pltpu.VMEM((n, width), BF16),
+            pltpu.VMEM((mesh_n[0], width), F32),
+            pltpu.VMEM((n, n), F32),
+            pltpu.VMEM((LANES, n), F32),
+            pltpu.VMEM((n, LANES), F32),
+            pltpu.VMEM((12, 8, n), F32),
+            pltpu.VMEM((2, 8, n), jnp.int32),
+            pltpu.VMEM((cols, win), F32),
+            pltpu.VMEM((cols, win), F32),
+        ],
+        compiler_params=pltpu.CompilerParams(vmem_limit_bytes=40 << 20),
+    )(sent, came)
+
+
+def fits(rows_n, cols_n, mol, width):
+    n = mol * rows_n * cols_n
+    two = rows_n >= 2 and cols_n >= 2 and not rows_n & (rows_n - 1) and not cols_n & (cols_n - 1)
+    return (two and 4 * n * n <= 24 << 20 and n % 512 == 0 and mol * rows_n % LANES == 0 and mol % 16 == 0
+            and mol * cols_n <= width and width % LANES == 0)
+
+
+def replicated(embedding, preference):
+    rows_n, cols_n = lax.axis_size("row"), lax.axis_size("col")
+    mol, width = embedding.shape[2:]
+    rows, cols = mol * cols_n, mol * rows_n
+    high = lax.reduce_precision(preference, 8, 7)
+    mid = lax.reduce_precision(preference - high, 8, 7)
+    tail = jnp.stack([high, mid, (preference - high) - mid]).astype(BF16)
+    tail = jnp.pad(tail, ((0, 5), (0, width - rows)))
+    held = jnp.concatenate([embedding.reshape(mol, width), tail], 0)
+    masks = [0]
+    for stage in stages(rows_n, cols_n):
+        came = [lax.ppermute(held, ("row", "col"), [(i, i ^ m) for i in range(rows_n * cols_n)]) for m in stage]
+        if len(masks) * 2 == rows_n * cols_n:
+            break
+        masks = masks + [m ^ a for m in stage for a in masks]
+        held = jnp.concatenate([held] + came, 0)
+    return tuple(compute(held, came[0], (rows_n, cols_n), mol, masks, rows, cols))
+
+
+def stages(rows_n, cols_n):
+    far = [m * 2 * cols_n + 1 for m in range(rows_n // 2 - 1, 0, -1)]
+    near = [m * 2 + 1 for m in range(cols_n - 1, 0, -1)]
+    return ([far] if far else []) + [near, [1]]
+
+
+def local(embedding, preference):
+    if fits(lax.axis_size("row"), lax.axis_size("col"), *embedding.shape[2:]):
+        return replicated(embedding, preference)
+    return tiled(embedding, preference)
 
 
 def broadcast(block, axis, source):
@@ -38,7 +314,7 @@
     return (first, second)
 
 
-def local(embedding, preference):
+def tiled(embedding, preference):
     rows_n = lax.axis_size("row")
     cols_n = lax.axis_size("col")
     row_idx = lax.axis_index("row")

time: 136 us -> 29.9 us (0.22)
  blocking collectives: 82.7 us -> 0 us
  waiting for transfers between devices: 30.4 us -> 10.1 us
  between operations: 14.9 us -> 0.7 us
  starting transfers between devices: 0.04 us -> 9.15 us
  Pallas kernels: 0 us -> 8.08 us
  other arithmetic: 4.63 us -> 0.71 us
  local copies, waits for them, and re-layouts: 2.77 us -> 0.87 us
    psum x2 -> x0, blocking collectives: 38.6 us -> none  [local(): colsum = lax.psum(jnp.sum(positive, axis=0), 'row')]
    all_gather x1 -> x0, blocking collectives: 32.4 us -> none  [local(): lax.all_gather(embedding, 'row', axis=1, tiled=True)]
    psum x1 -> x0, waiting for transfers between devices: 30.3 us -> none  [broadcast(): return lax.psum(block, axis)]
    unnamed x2 -> x0, blocking collectives: 11.7 us -> none
    ppermute x0 -> x7, waiting for transfers between devices: none -> 10.1 us  [replicated(): lax.ppermute(held, ('row', 'col'), [(i, i ^ m) for i in range(rows_n * co...]
    ppermute x0 -> x7, starting transfers between devices: none -> 9.15 us  [replicated(): lax.ppermute(held, ('row', 'col'), [(i, i ^ m) for i in range(rows_n * co...]
    pallas_call x0 -> x1, Pallas kernels: none -> 8.08 us  [compute(): pl.pallas_call(functools.partial(kernel, mesh_n, mol, masks, rows, cols,...]
    reduce_sum x8 -> x0, other arithmetic: 1.99 us -> none  [the longest x1 1.08 us: similarity(): row_sq = jnp.sum(row_vals * row_vals, axis=1)]
  transfers between devices with their start and end apart: 1 -> 7, of which waited for: 1 -> 5; matrix products, arithmetic and copies ran while one was open for 1% -> 0% of each run, Pallas kernels for 0% -> 0%
where the time goes in v2:
time: 29.9 us; the launch traced here: 29.6 us
  waiting for transfers between devices  10.1 us (34%)
  starting transfers between devices  9.15 us (31%)
  Pallas kernels  8.08 us (27%)
  local copies, waits for them, and re-layouts  0.87 us (3%)
  other arithmetic  0.71 us (2%)
  between operations  0.7 us (2%)
    ppermute x7, waiting for transfers between devices, replicated(): lax.ppermute(held, ('row', 'col'), [(i, i ^ m) for i in range(rows_n * co...  10.1 us
    ppermute x7, starting transfers between devices, replicated(): lax.ppermute(held, ('row', 'col'), [(i, i ^ m) for i in range(rows_n * co...  9.15 us
    pallas_call x1, Pallas kernels, compute(): pl.pallas_call(functools.partial(kernel, mesh_n, mol, masks, rows, cols,...  8.08 us
    unnamed x7, local copies, waits for them, and re-layouts  0.84 us
    another operation x1, other arithmetic  0.69 us
  transfers between devices with their start and end apart: 7, of which 5 were waited for; matrix products, arithmetic and copies ran while one was open for 0% of the time, Pallas kernels for 0%

profile of v2, /device:TPU:0, one launch (start us, length us, event | category | flops | bytes accessed | tf_op | source)
XLA Modules:
  0.0 29.6 jit_solution(4039416666799672686)
XLA Ops:
  0.6 0.7 %reduce-precision_convert_fusion.1 = (bf16[192]{0:T(256)(128)(2,1)S(1)}, bf16[192]{0:T(256)(128)(2,1)S(1)}, bf16[192]{0:T(256)(128)(2,1)S(1)}) fusion(f32[192]{0:T(256)} %param.3), kind=kLoop, calls=%fused_computation.28 | loop fusion | flops 1344 | bytes 1920 | tf_op jit(solution)/shard_map/convert.5
  1.3 0.0 copy-start
  1.3 0.8 %constant_dynamic-update-slice_fusion.4 = (bf16[224,256]{1,0:T(8,128)(2,1)S(1)}, bf16[896,256]{1,0:T(8,128)(2,1)S(1)}) fusion(bf16[1,1,48,256]{3,2,1,0:T(8,128)(2,1)} %param.2), kind=kLoop, calls=%fused_computation.5 | loop fusion | bytes 73728
  2.2 0.0 copy-done
  2.2 4.6 %collective-permute-start = (bf16[56,256]{1,0:T(8,128)(2,1)S(1)}, bf16[56,256]{1,0:T(8,128)(2,1)S(1)}, u32[]{:S(2)}, u32[]{:S(2)}) collective-permute-start(bf16[56,256]{1,0:T(8,128)(2,1)S(1)} %pad_maximum_fusion), channel_id=1, source_target_pairs={{0,25},{1,24},{2,27},{3,26},{4,29},{5,28},{6,31},{7,30},{8,17},{9,... | collective-permute-start | bytes 86024 | tf_op jit(solution)/shard_map/ppermute | solution.py:268
  6.7 0.0 collective-permute-start.2
  6.8 0.9 %collective-permute-start.1 = (bf16[56,256]{1,0:T(8,128)(2,1)S(1)}, bf16[56,256]{1,0:T(8,128)(2,1)S(1)}, u32[]{:S(2)}, u32[]{:S(2)}) collective-permute-start(bf16[56,256]{1,0:T(8,128)(2,1)S(1)} %pad_maximum_fusion), channel_id=1, source_target_pairs={{0,17},{1,16},{2,19},{3,18},{4,21},{5,20},{6,23},{7,22},{8,25},{9,... | collective-permute-start | bytes 86024 | tf_op jit(solution)/shard_map/ppermute | solution.py:268
  7.7 0.8 %collective-permute-done = bf16[56,256]{1,0:T(8,128)(2,1)S(1)} collective-permute-done((bf16[56,256]{1,0:T(8,128)(2,1)S(1)}, bf16[56,256]{1,0:T(8,128)(2,1)S(1)}, u32[]{:S(2)}, u32[]{:S(2)}) %collective-permute-start) | collective-permute-done | bytes 28704 | tf_op jit(solution)/shard_map/ppermute | solution.py:268
  8.4 2.6 %collective-permute-done.1 = bf16[56,256]{1,0:T(8,128)(2,1)S(1)} collective-permute-done((bf16[56,256]{1,0:T(8,128)(2,1)S(1)}, bf16[56,256]{1,0:T(8,128)(2,1)S(1)}, u32[]{:S(2)}, u32[]{:S(2)}) %collective-permute-start.1) | collective-permute-done | bytes 28704 | tf_op jit(solution)/shard_map/ppermute | solution.py:268
  11.1 0.0 collective-permute-done.2
  11.1 2.7 %collective-permute-start.3 = (bf16[224,256]{1,0:T(8,128)(2,1)S(1)}, bf16[224,256]{1,0:T(8,128)(2,1)S(1)}, u32[]{:S(2)}, u32[]{:S(2)}) collective-permute-start(bf16[224,256]{1,0:T(8,128)(2,1)S(1)} %get-tuple-element.2), channel_id=1, source_target_pairs={{0,7},{1,6},{2,5},{3,4},{4,3},{5,2},{6,1},{7,0},{8,15},{9,14},{10,... | collective-permute-start | bytes 344072 | tf_op jit(solution)/shard_map/ppermute | solution.py:268
  13.8 0.1 collective-permute-start.5
  13.8 0.7 %collective-permute-start.4 = (bf16[224,256]{1,0:T(8,128)(2,1)S(1)}, bf16[224,256]{1,0:T(8,128)(2,1)S(1)}, u32[]{:S(2)}, u32[]{:S(2)}) collective-permute-start(bf16[224,256]{1,0:T(8,128)(2,1)S(1)} %get-tuple-element.2), channel_id=1, source_target_pairs={{0,5},{1,4},{2,7},{3,6},{4,1},{5,0},{6,3},{7,2},{8,13},{9,12},{10,... | collective-permute-start | bytes 344072 | tf_op jit(solution)/shard_map/ppermute | solution.py:268
  14.5 2.7 %collective-permute-done.3 = bf16[224,256]{1,0:T(8,128)(2,1)S(1)} collective-permute-done((bf16[224,256]{1,0:T(8,128)(2,1)S(1)}, bf16[224,256]{1,0:T(8,128)(2,1)S(1)}, u32[]{:S(2)}, u32[]{:S(2)}) %collective-permute-start.3) | collective-permute-done | bytes 114720 | tf_op jit(solution)/shard_map/ppermute | solution.py:268
  17.3 2.4 %collective-permute-done.4 = bf16[224,256]{1,0:T(8,128)(2,1)S(1)} collective-permute-done((bf16[224,256]{1,0:T(8,128)(2,1)S(1)}, bf16[224,256]{1,0:T(8,128)(2,1)S(1)}, u32[]{:S(2)}, u32[]{:S(2)}) %collective-permute-start.4) | collective-permute-done | bytes 114720 | tf_op jit(solution)/shard_map/ppermute | solution.py:268
  19.6 0.0 collective-permute-done.5
  19.7 0.2 collective-permute-start.6
  19.9 1.7 %collective-permute-done.6.came_ref = bf16[896,256]{1,0:T(8,128)(2,1)S(1)} collective-permute-done((bf16[896,256]{1,0:T(8,128)(2,1)S(1)}, bf16[896,256]{1,0:T(8,128)(2,1)S(1)}, u32[]{:S(2)}, u32[]{:S(2)}) %collective-permute-start.6) | collective-permute-done | bytes 458784 | tf_op jit(solution)/shard_map/ppermute | solution.py:268
  21.6 8.1 %shard_map.41 = (f32[192,384]{1,0:T(8,128)}, f32[192,384]{1,0:T(8,128)}) custom-call(bf16[896,256]{1,0:T(8,128)(2,1)S(1)} %constant_dynamic-update-slice_fusion.5.sent_ref, bf16[896,256]{1,0:T(8,128)(2,1)S(1)} %collective-permute-done.6.came_ref), custom_call_target="tpu_custom_call" | custom-call | tf_op jit(solution)/shard_map/pallas_call | solution.py:230
  (11 shorter events, 0.1 us)
Async XLA Ops:
  1.3 0.8 %copy-start = (bf16[1,1,48,256]{3,2,1,0:T(8,128)(2,1)S(1)}, bf16[1,1,48,256]{3,2,1,0:T(8,128)(2,1)}, u32[]{:S(2)}) copy-start(bf16[1,1,48,256]{3,2,1,0:T(8,128)(2,1)} %param.2) | copy-start | bytes 73732
  2.2 6.2 %collective-permute-start = (bf16[56,256]{1,0:T(8,128)(2,1)S(1)}, bf16[56,256]{1,0:T(8,128)(2,1)S(1)}, u32[]{:S(2)}, u32[]{:S(2)}) collective-permute-start(bf16[56,256]{1,0:T(8,128)(2,1)S(1)} %pad_maximum_fusion), channel_id=1, source_target_pairs={{0,25},{1,24},{2,27},{3,26},{4,29},{5,28},{6,31},{7,30},{8,17},{9,... | collective-permute-start | bytes 86024 | tf_op jit(solution)/shard_map/ppermute | solution.py:268
  6.7 4.3 %collective-permute-start.2 = (bf16[56,256]{1,0:T(8,128)(2,1)S(1)}, bf16[56,256]{1,0:T(8,128)(2,1)S(1)}, u32[]{:S(2)}, u32[]{:S(2)}) collective-permute-start(bf16[56,256]{1,0:T(8,128)(2,1)S(1)} %pad_maximum_fusion), channel_id=1, source_target_pairs={{0,9},{1,8},{2,11},{3,10},{4,13},{5,12},{6,15},{7,14},{8,1},{9,0},... | collective-permute-start | bytes 86024 | tf_op jit(solution)/shard_map/ppermute | solution.py:268
  6.8 4.3 %collective-permute-start.1 = (bf16[56,256]{1,0:T(8,128)(2,1)S(1)}, bf16[56,256]{1,0:T(8,128)(2,1)S(1)}, u32[]{:S(2)}, u32[]{:S(2)}) collective-permute-start(bf16[56,256]{1,0:T(8,128)(2,1)S(1)} %pad_maximum_fusion), channel_id=1, source_target_pairs={{0,17},{1,16},{2,19},{3,18},{4,21},{5,20},{6,23},{7,22},{8,25},{9,... | collective-permute-start | bytes 86024 | tf_op jit(solution)/shard_map/ppermute | solution.py:268
  11.1 6.2 %collective-permute-start.3 = (bf16[224,256]{1,0:T(8,128)(2,1)S(1)}, bf16[224,256]{1,0:T(8,128)(2,1)S(1)}, u32[]{:S(2)}, u32[]{:S(2)}) collective-permute-start(bf16[224,256]{1,0:T(8,128)(2,1)S(1)} %get-tuple-element.2), channel_id=1, source_target_pairs={{0,7},{1,6},{2,5},{3,4},{4,3},{5,2},{6,1},{7,0},{8,15},{9,14},{10,... | collective-permute-start | bytes 344072 | tf_op jit(solution)/shard_map/ppermute | solution.py:268
  13.8 5.9 %collective-permute-start.5 = (bf16[224,256]{1,0:T(8,128)(2,1)S(1)}, bf16[224,256]{1,0:T(8,128)(2,1)S(1)}, u32[]{:S(2)}, u32[]{:S(2)}) collective-permute-start(bf16[224,256]{1,0:T(8,128)(2,1)S(1)} %get-tuple-element.2), channel_id=1, source_target_pairs={{0,3},{1,2},{2,1},{3,0},{4,7},{5,6},{6,5},{7,4},{8,11},{9,10},{10,... | collective-permute-start | bytes 344072 | tf_op jit(solution)/shard_map/ppermute | solution.py:268
  13.8 5.8 %collective-permute-start.4 = (bf16[224,256]{1,0:T(8,128)(2,1)S(1)}, bf16[224,256]{1,0:T(8,128)(2,1)S(1)}, u32[]{:S(2)}, u32[]{:S(2)}) collective-permute-start(bf16[224,256]{1,0:T(8,128)(2,1)S(1)} %get-tuple-element.2), channel_id=1, source_target_pairs={{0,5},{1,4},{2,7},{3,6},{4,1},{5,0},{6,3},{7,2},{8,13},{9,12},{10,... | collective-permute-start | bytes 344072 | tf_op jit(solution)/shard_map/ppermute | solution.py:268
  19.7 1.9 %collective-permute-start.6 = (bf16[896,256]{1,0:T(8,128)(2,1)S(1)}, bf16[896,256]{1,0:T(8,128)(2,1)S(1)}, u32[]{:S(2)}, u32[]{:S(2)}) collective-permute-start(bf16[896,256]{1,0:T(8,128)(2,1)S(1)} %constant_dynamic-update-slice_fusion.5.sent_ref), channel_id=1, source_target_pairs={{0,1},{1,0},{2,3},{3,2},{4,5},{5,4},{6,7},{7,6},{8,9},{9,8},{10,11... | collective-permute-start | bytes 1376264 | tf_op jit(solution)/shard_map/ppermute | solution.py:268

commit v3 on v2

--- a/solution.py
+++ b/solution.py
@@ -52,30 +52,31 @@
         q_ref[s:s + step, :] = jnp.dot(jnp.concatenate([high, low], 1), ones, preferred_element_type=F32)
 
 
-def unpack(mesh_n, mol, masks, me, halves, x_ref, pref_ref):
+def unpack(mesh_n, mol, owners, me, pieces, x_ref, pref_ref):
     rows_n, cols_n = mesh_n
     seen = set()
-    for half, flip in zip(halves, (0, 1)):
+    for piece, masks in zip(pieces, owners):
         for p, mask in enumerate(masks):
-            owner = me ^ (mask ^ flip)
+            owner = me ^ mask
             row, col = owner // cols_n, owner % cols_n
             at = p * (mol + 8)
-            x_ref[pl.ds(pl.multiple_of((col * rows_n + row) * mol, 16), mol), :] = half[at:at + mol, :]
-            if (mask ^ flip) // cols_n not in seen:
-                seen.add((mask ^ flip) // cols_n)
-                tail = half[at + mol:at + mol + 8, :].astype(F32)
+            x_ref[pl.ds(pl.multiple_of((col * rows_n + row) * mol, 16), mol), :] = piece[at:at + mol, :]
+            if mask // cols_n not in seen:
+                seen.add(mask // cols_n)
+                tail = piece[at + mol:at + mol + 8, :].astype(F32)
                 pref_ref[pl.ds(row, 1), :] = (tail[0:1] + tail[1:2]) + tail[2:3]
 
 
 FIRST, GAIN, OWN, R1D, ONE, TWO, BASE, Z, R2D, AV1D, STAR, WZ = range(12)
 
 
-def kernel(mesh_n, mol, masks, rows, cols, win, sent_ref, came_ref, resp_ref, avail_ref, x_ref, pref_ref, g_ref, c_ref, q_ref, row_ref, k_ref, r_out, a_out,
-           T=512, R=256, CH=128, QS=256):
+def kernel(mesh_n, mol, owners, rows, cols, win, *refs, T=512, R=256, QS=256):
+    pieces, refs = refs[:len(owners)], refs[len(owners):]
+    resp_ref, avail_ref, x_ref, pref_ref, g_ref, c_ref, a_ref, q_ref, row_ref, k_ref, r_out, a_out, t_ref, out_sem = refs
     n, width = x_ref.shape
     rows_n, cols_n = mesh_n
     row_idx, col_idx = lax.axis_index("row"), lax.axis_index("col")
-    unpack(mesh_n, mol, masks, row_idx * cols_n + col_idx, (sent_ref, came_ref), x_ref, pref_ref)
+    unpack(mesh_n, mol, owners, row_idx * cols_n + col_idx, pieces, x_ref, pref_ref)
     squares(x_ref, q_ref, QS)
     sub8 = lax.broadcasted_iota(jnp.int32, (8, LANES), 0)
     lane8 = lax.broadcasted_iota(jnp.int32, (8, LANES), 1)
@@ -117,57 +118,65 @@
             row_ref[R1D, :, lanes] = 0.5 * (own - jnp.where(own == first, second, first))
             k_ref[0, :, lanes] = a
             k_ref[1, :, lanes] = a - sub8
-            row_ref[ONE, :, lanes] = low8
-            row_ref[TWO, :, lanes] = low8
     H = -(-blocks // 16) * 16
     subL = lax.broadcasted_iota(jnp.int32, (LANES, LANES), 0)
     subH = lax.broadcasted_iota(jnp.int32, (H, LANES), 0)
-    short, tall = [[], [], []], []
+    short, diag, tall, eyes = [[], [], []], [[], [], []], [], []
+    eye = jnp.where(subL == lax.broadcasted_iota(jnp.int32, (LANES, LANES), 1), 1.0, 0.0).astype(BF16)
     for l in range(blocks):
         lanes = slice(l * LANES, (l + 1) * LANES)
         k = k_ref[0, 0:1, lanes]
+        eyes.append(eye)
+        for i, part in enumerate(thirds(0.5 * row_ref[R1D, 0:1, lanes])):
+            diag[i].append(jnp.where(subH == l, part, 0.0).astype(BF16))
         tall.append(jnp.where(subL == k % LANES, 1.0, 0.0).astype(BF16))
         for i, part in enumerate(thirds(row_ref[GAIN, 0:1, lanes])):
             short[i].append(jnp.where(subH == k // LANES, part, 0.0).astype(BF16))
-    tall = jnp.concatenate(tall, 1)
+    tall, eyes = jnp.concatenate(tall, 1), jnp.concatenate(eyes, 1)
     short = jnp.concatenate([jnp.concatenate(s, 1) for s in short], 0)
+    diag = jnp.concatenate([jnp.concatenate(s, 1) for s in diag], 0)
     s = lax.dot_general(short, tall, NT, preferred_element_type=F32)
     s = (s[0:H] + s[H:2 * H]) + s[2 * H:]
+    side = lax.dot_general(jnp.concatenate([tall, eyes], 1), jnp.concatenate([short, diag], 1), NT, preferred_element_type=F32)
+    side = (side[:, 0:H] + side[:, H:2 * H]) + side[:, 2 * H:]
     half = []
     for l in range(blocks):
         lanes = slice(l * LANES, (l + 1) * LANES)
+        c = jnp.broadcast_to(side[:, l:l + 1], (LANES, LANES))
+        c_ref[:, lanes] = c
+        a_ref[:, lanes] = jnp.minimum(c, 0.0)
         av = s[l:l + 1, :]
         row_ref[AV1D, :, lanes] = jnp.broadcast_to(av, (8, LANES))
         half.append(av + 0.5 * row_ref[R1D, 0:1, lanes])
     half = jnp.concatenate(half + [jnp.zeros((H - blocks, LANES), F32)] * (H > blocks), 0)
-    half = jnp.concatenate(thirds(half), 0)
-    got = jnp.dot(half.astype(BF16), tall, preferred_element_type=F32)
+    half = jnp.concatenate(thirds(half), 0).astype(BF16)
+    got = jnp.dot(half, tall, preferred_element_type=F32)
     got = (got[0:H] + got[H:2 * H]) + got[2 * H:]
-    pick = lax.broadcasted_iota(jnp.int32, (3 * H, n), 0) % H == lax.broadcasted_iota(jnp.int32, (3 * H, n), 1) // LANES
-    side = jnp.concatenate([half, jnp.zeros((LANES - 3 * H, LANES), F32)], 0).T[:, 0:3 * H].astype(BF16)
-    c_ref[...] = jnp.dot(side, jnp.where(pick, 1.0, 0.0).astype(BF16), preferred_element_type=F32)
     for l in range(blocks):
         lanes = slice(l * LANES, (l + 1) * LANES)
         k = k_ref[0, 0:1, lanes]
         c = jnp.sum(jnp.where(subH == k // LANES, got[:, lanes], 0.0), axis=0, keepdims=True)
         row_ref[WZ, :, lanes] = jnp.broadcast_to(c, (8, LANES))
-    def tops(j, _):
-        groups = CH // 8
-        a = [jnp.minimum(c_ref[8 * r:8 * r + 8, pl.ds(pl.multiple_of(j * LANES, LANES), LANES)], 0.0) for r in range(groups)]
-        at = [pl.ds(pl.multiple_of(j * CH + 8 * r, 8), 8) for r in range(groups)]
-        for l in range(blocks):
-            k = slice(l * LANES, (l + 1) * LANES)
-            star = k_ref[1, :, k] - j * CH
-            one, two = row_ref[ONE, :, k], row_ref[TWO, :, k]
-            for r in range(groups):
-                one, two = push(one, two, jnp.where(star == 8 * r, LOW, g_ref[at[r], k] + a[r]))
-            row_ref[ONE, :, k] = one
-            row_ref[TWO, :, k] = two
-        return 0
-    lax.fori_loop(0, n // CH, tops, 0)
+    for t in range(0, n, T):
+        K = T // LANES
+        lanes = [slice(t + l * LANES, t + (l + 1) * LANES) for l in range(K)]
+        star = [k_ref[1, :, k] for k in lanes]
+        def tops(j, tops):
+            one, two = list(tops[:K]), list(tops[K:])
+            base = pl.multiple_of(j * LANES, LANES)
+            near = [s - base for s in star]
+            for r in range(0, LANES, 8):
+                a = a_ref[r:r + 8, pl.ds(base, LANES)]
+                for l, k in enumerate(lanes):
+                    u = jnp.where(near[l] == r, LOW, g_ref[pl.ds(pl.multiple_of(base + r, 8), 8), k] + a)
+                    one[l], two[l] = push(one[l], two[l], u)
+            return one + two
+        ends = lax.fori_loop(0, blocks, tops, [low8] * (2 * K))
+        for l, k in enumerate(lanes):
+            row_ref[ONE, :, k], row_ref[TWO, :, k], _ = fold(ends[l], ends[K + l])
     for l in range(blocks):
         k = slice(l * LANES, (l + 1) * LANES)
-        one, two, _ = fold(row_ref[ONE, :, k], row_ref[TWO, :, k])
+        one, two = row_ref[ONE, :, k], row_ref[TWO, :, k]
         own, r1d, first, gain, av1d = (row_ref[i, :, k] for i in (OWN, R1D, FIRST, GAIN, AV1D))
         t = jnp.minimum(row_ref[WZ, :, k] - gain, 0.0)
         star = row_ref[STAR, :, k] + t
@@ -182,14 +191,13 @@
         row_ref[WZ, :, k] = (4 / 3) * gain + jnp.where(star == one, z, 0.0)
         row_ref[STAR, :, k] = t
     r0, c0 = row_idx * rows, col_idx * cols
+    off = pl.multiple_of(r0 % LANES, 8)
     w0 = pl.multiple_of((r0 // LANES) * LANES, LANES)
-    def body4(j, _):
+    def block(j):
         st = pl.multiple_of(c0 + j * LANES, LANES)
         groups = LANES // 8
         at = [pl.ds(pl.multiple_of(st + 8 * r, 8), 8) for r in range(groups)]
-        out = [pl.ds(pl.multiple_of(j * LANES + 8 * r, 8), 8) for r in range(groups)]
-        c = [c_ref[8 * r:8 * r + 8, pl.ds(st, LANES)] for r in range(groups)]
-        a = [jnp.minimum(v, 0.0) for v in c]
+        a = [a_ref[8 * r:8 * r + 8, pl.ds(st, LANES)] for r in range(groups)]
         r2d = (4 / 3) * row_ref[R2D, :, pl.ds(st, LANES)]
         acc = [jnp.where(gap == 8 * r, r2d, 0.0) for r in range(groups)]
         def resp2(r, k, star, row):
@@ -213,70 +221,105 @@
                 t = jnp.where(star == 8 * r, ts, a[r])
                 a2 = 0.5 * t + jnp.minimum(cs[r] - 0.5 * jnp.maximum(r2, 0.0), 0.0)
                 dg = gap == st + 8 * r - (w0 + l)
-                r_out[out[r], l:l + LANES] = jnp.where(dg, rd, r2)
-                a_out[out[r], l:l + LANES] = jnp.where(dg, 0.5 * ad + (cs[r] - 0.5 * rd), a2)
-        return 0
-    lax.fori_loop(0, cols // LANES, body4, 0)
-    off = pl.multiple_of(r0 - w0, 8)
-    g_ref[0:win, 0:cols] = r_out[...].T
-    g_ref[win:2 * win, 0:cols] = a_out[...].T
-    resp_ref[...] = g_ref[pl.ds(off, rows), 0:cols]
-    avail_ref[...] = g_ref[pl.ds(win + off, rows), 0:cols]
-
-
-def compute(sent, came, mesh_n, mol, masks, rows, cols):
-    n, width = mol * mesh_n[0] * mesh_n[1], sent.shape[1]
+                r_out[8 * r:8 * r + 8, j * win + l:j * win + l + LANES] = jnp.where(dg, rd, r2)
+                a_out[8 * r:8 * r + 8, j * win + l:j * win + l + LANES] = jnp.where(dg, 0.5 * ad + (cs[r] - 0.5 * rd), a2)
+        lanes = slice(j * LANES, (j + 1) * LANES)
+        for i, (tile, out_ref) in enumerate(((r_out, resp_ref), (a_out, avail_ref))):
+            t_ref[i, :, lanes] = tile[:, j * win:(j + 1) * win].T
+            copy = pltpu.make_async_copy(t_ref.at[i, pl.ds(off, rows), lanes], out_ref.at[:, lanes], out_sem.at[j, i])
+            copy.start()
+            copies.append(copy)
+    copies = []
+    for j in range(cols // LANES):
+        block(j)
+    for copy in copies:
+        copy.wait()
+
+
+def compute(pieces, mesh_n, mol, owners, rows, cols):
+    n, width = mol * mesh_n[0] * mesh_n[1], pieces[0].shape[1]
     win = -(-(rows + LANES - math.gcd(rows, LANES)) // LANES) * LANES
     return pl.pallas_call(
-        functools.partial(kernel, mesh_n, mol, masks, rows, cols, win),
+        functools.partial(kernel, mesh_n, mol, owners, rows, cols, win),
         out_shape=[jax.ShapeDtypeStruct((rows, cols), F32)] * 2,
-        in_specs=[pl.BlockSpec(memory_space=pltpu.VMEM)] * 2,
-        out_specs=[pl.BlockSpec(memory_space=pltpu.VMEM)] * 2,
+        in_specs=[pl.BlockSpec(memory_space=pltpu.VMEM)] * len(pieces),
+        out_specs=[pl.BlockSpec(memory_space=pl.ANY)] * 2,
         scratch_shapes=[
             pltpu.VMEM((n, width), BF16),
             pltpu.VMEM((mesh_n[0], width), F32),
             pltpu.VMEM((n, n), F32),
             pltpu.VMEM((LANES, n), F32),
+            pltpu.VMEM((LANES, n), F32),
             pltpu.VMEM((n, LANES), F32),
             pltpu.VMEM((12, 8, n), F32),
             pltpu.VMEM((2, 8, n), jnp.int32),
-            pltpu.VMEM((cols, win), F32),
-            pltpu.VMEM((cols, win), F32),
+            pltpu.VMEM((LANES, cols // LANES * win), F32),
+            pltpu.VMEM((LANES, cols // LANES * win), F32),
+            pltpu.VMEM((2, win, cols), F32),
+            pltpu.SemaphoreType.DMA((cols // LANES, 2)),
         ],
         compiler_params=pltpu.CompilerParams(vmem_limit_bytes=40 << 20),
-    )(sent, came)
+    )(*pieces)
+
+
+def pack_kernel(mol, embedding_ref, preference_ref, out_ref, e_ref, p_ref, sems):
+    copies = [
+        pltpu.make_async_copy(preference_ref, p_ref, sems.at[0]),
+        pltpu.make_async_copy(embedding_ref, e_ref, sems.at[1]),
+    ]
+    for copy in copies:
+        copy.start()
+    for copy in copies:
+        copy.wait()
+    out_ref[0:mol, :] = e_ref[...]
+    values = p_ref[...]
+    fill = jnp.zeros((1, out_ref.shape[1] - values.shape[1]), F32)
+    parts = [jnp.concatenate([part, fill], 1) for part in thirds(values)]
+    out_ref[mol:mol + 8, :] = jnp.concatenate(parts + [jnp.zeros((5, out_ref.shape[1]), F32)], 0).astype(BF16)
+
+
+def pack(embedding, preference):
+    mol, width = embedding.shape
+    return pl.pallas_call(
+        functools.partial(pack_kernel, mol),
+        out_shape=pltpu.VMEM((mol + 8, width), BF16),
+        in_specs=[pl.BlockSpec(memory_space=pltpu.HBM)] * 2,
+        out_specs=pl.BlockSpec(memory_space=pltpu.VMEM),
+        scratch_shapes=[pltpu.VMEM((mol, width), BF16), pltpu.VMEM(preference.shape, F32), pltpu.SemaphoreType.DMA((2,))],
+        compiler_params=pltpu.CompilerParams(vmem_limit_bytes=60 << 20),
+    )(embedding, preference)
 
 
 def fits(rows_n, cols_n, mol, width):
     n = mol * rows_n * cols_n
     two = rows_n >= 2 and cols_n >= 2 and not rows_n & (rows_n - 1) and not cols_n & (cols_n - 1)
-    return (two and 4 * n * n <= 24 << 20 and n % 512 == 0 and mol * rows_n % LANES == 0 and mol % 16 == 0
+    return (two and 4 * n * n <= 16 << 20 and n % 512 == 0 and mol * rows_n % LANES == 0 and mol % 16 == 0
             and mol * cols_n <= width and width % LANES == 0)
+
+
+def stages(rows_n, cols_n):
+    far = [m * 2 * cols_n + 1 for m in range(1,rows_n//2)]
+    near = [m * 2 + 1 for m in range(1,cols_n)]
+    return far, near
+
+
+def swap(block, mask):
+    size = lax.axis_size("row") * lax.axis_size("col")
+    return lax.ppermute(block, ("row", "col"), [(i, i ^ mask) for i in range(size)])
 
 
 def replicated(embedding, preference):
     rows_n, cols_n = lax.axis_size("row"), lax.axis_size("col")
     mol, width = embedding.shape[2:]
     rows, cols = mol * cols_n, mol * rows_n
-    high = lax.reduce_precision(preference, 8, 7)
-    mid = lax.reduce_precision(preference - high, 8, 7)
-    tail = jnp.stack([high, mid, (preference - high) - mid]).astype(BF16)
-    tail = jnp.pad(tail, ((0, 5), (0, width - rows)))
-    held = jnp.concatenate([embedding.reshape(mol, width), tail], 0)
-    masks = [0]
-    for stage in stages(rows_n, cols_n):
-        came = [lax.ppermute(held, ("row", "col"), [(i, i ^ m) for i in range(rows_n * cols_n)]) for m in stage]
-        if len(masks) * 2 == rows_n * cols_n:
-            break
-        masks = masks + [m ^ a for m in stage for a in masks]
-        held = jnp.concatenate([held] + came, 0)
-    return tuple(compute(held, came[0], (rows_n, cols_n), mol, masks, rows, cols))
-
-
-def stages(rows_n, cols_n):
-    far = [m * 2 * cols_n + 1 for m in range(rows_n // 2 - 1, 0, -1)]
-    near = [m * 2 + 1 for m in range(cols_n - 1, 0, -1)]
-    return ([far] if far else []) + [near, [1]]
+    held = pack(embedding.reshape(mol, width), preference.reshape(1, rows))
+    far, near = stages(rows_n, cols_n)
+    line = jnp.concatenate([held] + [swap(held, m) for m in far], 0)
+    pieces = [line] + [swap(line, m) for m in near]
+    owners = [[n ^ f for f in [0] + far] for n in [0] + near]
+    pieces = pieces + [swap(piece, 1) for piece in pieces]
+    owners = owners + [[m ^ 1 for m in masks] for masks in owners]
+    return tuple(compute(pieces, (rows_n, cols_n), mol, owners, rows, cols))
 
 
 def local(embedding, preference):

time: 29.9 us -> 28.7 us (0.960)
  local copies, waits for them, and re-layouts: 0.87 us -> 0 us
  other arithmetic: 0.71 us -> 0.01 us
  starting transfers between devices: 9.15 us -> 9.62 us
  Pallas kernels: 8.08 us -> 8.54 us
  waiting for transfers between devices: 10.1 us -> 9.71 us
    unnamed x7 -> x0, local copies, waits for them, and re-layouts: 0.84 us -> none
    another operation x1 -> x0, other arithmetic: 0.69 us -> none
    ppermute x7 -> x10, starting transfers between devices: 9.15 us -> 9.62 us  [swap(): lax.ppermute(block, ('row', 'col'), [(i, i ^ mask) for i in range(size)])]
    pallas_call x1 -> x2, Pallas kernels: 8.08 us -> 8.54 us  [the longest x1 7.74 us: compute(): pl.pallas_call(functools.partial(kernel, mesh_n, mol, owners, rows, cols,...]
    ppermute x7 -> x10, waiting for transfers between devices: 10.1 us -> 9.71 us  [swap(): lax.ppermute(block, ('row', 'col'), [(i, i ^ mask) for i in range(size)])]
  transfers between devices with their start and end apart: 7 -> 10, of which waited for: 5 -> 6; matrix products, arithmetic and copies ran while one was open for 0% -> 0% of each run, Pallas kernels for 0% -> 0%
where the time goes in v3:
time: 28.7 us; the launch traced here: 28.5 us
  waiting for transfers between devices  9.71 us (34%)
  starting transfers between devices  9.62 us (34%)
  Pallas kernels  8.54 us (30%)
  between operations  0.65 us (2%)
    ppermute x10, waiting for transfers between devices, swap(): lax.ppermute(block, ('row', 'col'), [(i, i ^ mask) for i in range(size)])  9.71 us
    ppermute x10, starting transfers between devices, swap(): lax.ppermute(block, ('row', 'col'), [(i, i ^ mask) for i in range(size)])  9.62 us
    pallas_call x1, Pallas kernels, compute(): pl.pallas_call(functools.partial(kernel, mesh_n, mol, owners, rows, cols,...  7.74 us
    pallas_call x1, Pallas kernels, pack(): pl.pallas_call(functools.partial(pack_kernel, mol), out_shape=pltpu.VMEM(...  0.79 us
  transfers between devices with their start and end apart: 10, of which 6 were waited for; matrix products, arithmetic and copies ran while one was open for 0% of the time, Pallas kernels for 0%

profile of v3, /device:TPU:0, one launch (start us, length us, event | category | flops | bytes accessed | tf_op | source)
XLA Modules:
  0.0 28.5 jit_solution(4262373982461962967)
XLA Ops:
  0.6 0.8 %shard_map.41 = bf16[56,256]{1,0:T(8,128)(2,1)S(1)} custom-call(bf16[48,256]{1,0:T(8,128)(2,1)} %bitcast.2, f32[1,192]{1,0:T(1,128)} %bitcast.3), custom_call_target="tpu_custom_call" | custom-call | tf_op jit(solution)/shard_map/pallas_call | solution.py:283
  1.4 4.6 %collective-permute-start.2 = (bf16[56,256]{1,0:T(8,128)(2,1)S(1)}, bf16[56,256]{1,0:T(8,128)(2,1)S(1)}, u32[]{:S(2)}, u32[]{:S(2)}) collective-permute-start(bf16[56,256]{1,0:T(8,128)(2,1)S(1)} %shard_map.41), channel_id=1, source_target_pairs={{0,25},{1,24},{2,27},{3,26},{4,29},{5,28},{6,31},{7,30},{8,17},{9,... | collective-permute-start | bytes 86024 | tf_op jit(solution)/shard_map/ppermute | solution.py:308
  6.0 0.0 collective-permute-start.1
  6.0 0.9 %collective-permute-start = (bf16[56,256]{1,0:T(8,128)(2,1)S(1)}, bf16[56,256]{1,0:T(8,128)(2,1)S(1)}, u32[]{:S(2)}, u32[]{:S(2)}) collective-permute-start(bf16[56,256]{1,0:T(8,128)(2,1)S(1)} %shard_map.41), channel_id=1, source_target_pairs={{0,9},{1,8},{2,11},{3,10},{4,13},{5,12},{6,15},{7,14},{8,1},{9,0},... | collective-permute-start | bytes 86024 | tf_op jit(solution)/shard_map/ppermute | solution.py:308
  6.9 0.8 %collective-permute-done.2 = bf16[56,256]{1,0:T(8,128)(2,1)S(1)} collective-permute-done((bf16[56,256]{1,0:T(8,128)(2,1)S(1)}, bf16[56,256]{1,0:T(8,128)(2,1)S(1)}, u32[]{:S(2)}, u32[]{:S(2)}) %collective-permute-start.2) | collective-permute-done | bytes 28704 | tf_op jit(solution)/shard_map/ppermute | solution.py:308
  7.7 2.8 %collective-permute-done.1 = bf16[56,256]{1,0:T(8,128)(2,1)S(1)} collective-permute-done((bf16[56,256]{1,0:T(8,128)(2,1)S(1)}, bf16[56,256]{1,0:T(8,128)(2,1)S(1)}, u32[]{:S(2)}, u32[]{:S(2)}) %collective-permute-start.1) | collective-permute-done | bytes 28704 | tf_op jit(solution)/shard_map/ppermute | solution.py:308
  10.4 0.0 collective-permute-done
  10.5 2.6 %collective-permute-start.5 = (bf16[224,256]{1,0:T(8,128)(2,1)S(1)}, bf16[224,256]{1,0:T(8,128)(2,1)S(1)}, u32[]{:S(2)}, u32[]{:S(2)}) collective-permute-start(bf16[224,256]{1,0:T(8,128)(2,1)S(1)} %pad_maximum_fusion.refs_0_), channel_id=1, source_target_pairs={{0,7},{1,6},{2,5},{3,4},{4,3},{5,2},{6,1},{7,0},{8,15},{9,14},{10,... | collective-permute-start | bytes 344072 | tf_op jit(solution)/shard_map/ppermute | solution.py:308
  13.0 0.2 collective-permute-start.4
  13.2 0.6 %collective-permute-start.3 = (bf16[224,256]{1,0:T(8,128)(2,1)S(1)}, bf16[224,256]{1,0:T(8,128)(2,1)S(1)}, u32[]{:S(2)}, u32[]{:S(2)}) collective-permute-start(bf16[224,256]{1,0:T(8,128)(2,1)S(1)} %pad_maximum_fusion.refs_0_), channel_id=1, source_target_pairs={{0,3},{1,2},{2,1},{3,0},{4,7},{5,6},{6,5},{7,4},{8,11},{9,10},{10,... | collective-permute-start | bytes 344072 | tf_op jit(solution)/shard_map/ppermute | solution.py:308
  13.8 0.1 collective-permute-start.6
  13.8 2.7 %collective-permute-done.5.refs_3_ = bf16[224,256]{1,0:T(8,128)(2,1)S(1)} collective-permute-done((bf16[224,256]{1,0:T(8,128)(2,1)S(1)}, bf16[224,256]{1,0:T(8,128)(2,1)S(1)}, u32[]{:S(2)}, u32[]{:S(2)}) %collective-permute-start.5) | collective-permute-done | bytes 114720 | tf_op jit(solution)/shard_map/ppermute | solution.py:308
  16.5 0.2 collective-permute-start.9
  16.8 2.5 %collective-permute-done.4.refs_2_ = bf16[224,256]{1,0:T(8,128)(2,1)S(1)} collective-permute-done((bf16[224,256]{1,0:T(8,128)(2,1)S(1)}, bf16[224,256]{1,0:T(8,128)(2,1)S(1)}, u32[]{:S(2)}, u32[]{:S(2)}) %collective-permute-start.4) | collective-permute-done | bytes 114720 | tf_op jit(solution)/shard_map/ppermute | solution.py:308
  19.3 0.1 collective-permute-start.8
  19.4 0.0 collective-permute-done.3.refs_1_
  19.4 0.4 %collective-permute-start.7 = (bf16[224,256]{1,0:T(8,128)(2,1)S(1)}, bf16[224,256]{1,0:T(8,128)(2,1)S(1)}, u32[]{:S(2)}, u32[]{:S(2)}) collective-permute-start(bf16[224,256]{1,0:T(8,128)(2,1)S(1)} %collective-permute-done.3.refs_1_), channel_id=1, source_target_pairs={{0,1},{1,0},{2,3},{3,2},{4,5},{5,4},{6,7},{7,6},{8,9},{9,8},{10,11... | collective-permute-start | bytes 344072 | tf_op jit(solution)/shard_map/ppermute | solution.py:308
  19.8 0.0 collective-permute-done.6.refs_4_
  19.8 0.0 collective-permute-done.9.refs_7_
  19.8 0.8 %collective-permute-done.8.refs_6_ = bf16[224,256]{1,0:T(8,128)(2,1)S(1)} collective-permute-done((bf16[224,256]{1,0:T(8,128)(2,1)S(1)}, bf16[224,256]{1,0:T(8,128)(2,1)S(1)}, u32[]{:S(2)}, u32[]{:S(2)}) %collective-permute-start.8) | collective-permute-done | bytes 114720 | tf_op jit(solution)/shard_map/ppermute | solution.py:308
  20.6 0.2 collective-permute-done.7.refs_5_
  20.8 7.7 %shard_map.42 = (f32[192,384]{1,0:T(8,128)}, f32[192,384]{1,0:T(8,128)}) custom-call(bf16[224,256]{1,0:T(8,128)(2,1)S(1)} %pad_maximum_fusion.refs_0_, bf16[224,256]{1,0:T(8,128)(2,1)S(1)} %collective-permute-done.3.refs_1_, bf16[224,256]{1,0:T(8,128)(2,1)S(1)} %collective-permute-done.4.refs_2_, bf16[224,256]{1,0:T(8,128)(2,1)S(1)} %collective-permute-done.5.refs_3_, ...), custom_call_target="tpu_custom_call" | custom-call | tf_op jit(solution)/shard_map/pallas_call | solution.py:242
  (1 shorter events, 0.0 us)
Async XLA Ops:
  1.4 6.2 %collective-permute-start.2 = (bf16[56,256]{1,0:T(8,128)(2,1)S(1)}, bf16[56,256]{1,0:T(8,128)(2,1)S(1)}, u32[]{:S(2)}, u32[]{:S(2)}) collective-permute-start(bf16[56,256]{1,0:T(8,128)(2,1)S(1)} %shard_map.41), channel_id=1, source_target_pairs={{0,25},{1,24},{2,27},{3,26},{4,29},{5,28},{6,31},{7,30},{8,17},{9,... | collective-permute-start | bytes 86024 | tf_op jit(solution)/shard_map/ppermute | solution.py:308
  6.0 4.5 %collective-permute-start.1 = (bf16[56,256]{1,0:T(8,128)(2,1)S(1)}, bf16[56,256]{1,0:T(8,128)(2,1)S(1)}, u32[]{:S(2)}, u32[]{:S(2)}) collective-permute-start(bf16[56,256]{1,0:T(8,128)(2,1)S(1)} %shard_map.41), channel_id=1, source_target_pairs={{0,17},{1,16},{2,19},{3,18},{4,21},{5,20},{6,23},{7,22},{8,25},{9,... | collective-permute-start | bytes 86024 | tf_op jit(solution)/shard_map/ppermute | solution.py:308
  6.0 4.5 %collective-permute-start = (bf16[56,256]{1,0:T(8,128)(2,1)S(1)}, bf16[56,256]{1,0:T(8,128)(2,1)S(1)}, u32[]{:S(2)}, u32[]{:S(2)}) collective-permute-start(bf16[56,256]{1,0:T(8,128)(2,1)S(1)} %shard_map.41), channel_id=1, source_target_pairs={{0,9},{1,8},{2,11},{3,10},{4,13},{5,12},{6,15},{7,14},{8,1},{9,0},... | collective-permute-start | bytes 86024 | tf_op jit(solution)/shard_map/ppermute | solution.py:308
  10.5 6.1 %collective-permute-start.5 = (bf16[224,256]{1,0:T(8,128)(2,1)S(1)}, bf16[224,256]{1,0:T(8,128)(2,1)S(1)}, u32[]{:S(2)}, u32[]{:S(2)}) collective-permute-start(bf16[224,256]{1,0:T(8,128)(2,1)S(1)} %pad_maximum_fusion.refs_0_), channel_id=1, source_target_pairs={{0,7},{1,6},{2,5},{3,4},{4,3},{5,2},{6,1},{7,0},{8,15},{9,14},{10,... | collective-permute-start | bytes 344072 | tf_op jit(solution)/shard_map/ppermute | solution.py:308
  13.0 6.3 %collective-permute-start.4 = (bf16[224,256]{1,0:T(8,128)(2,1)S(1)}, bf16[224,256]{1,0:T(8,128)(2,1)S(1)}, u32[]{:S(2)}, u32[]{:S(2)}) collective-permute-start(bf16[224,256]{1,0:T(8,128)(2,1)S(1)} %pad_maximum_fusion.refs_0_), channel_id=1, source_target_pairs={{0,5},{1,4},{2,7},{3,6},{4,1},{5,0},{6,3},{7,2},{8,13},{9,12},{10,... | collective-permute-start | bytes 344072 | tf_op jit(solution)/shard_map/ppermute | solution.py:308
  13.2 6.2 %collective-permute-start.3 = (bf16[224,256]{1,0:T(8,128)(2,1)S(1)}, bf16[224,256]{1,0:T(8,128)(2,1)S(1)}, u32[]{:S(2)}, u32[]{:S(2)}) collective-permute-start(bf16[224,256]{1,0:T(8,128)(2,1)S(1)} %pad_maximum_fusion.refs_0_), channel_id=1, source_target_pairs={{0,3},{1,2},{2,1},{3,0},{4,7},{5,6},{6,5},{7,4},{8,11},{9,10},{10,... | collective-permute-start | bytes 344072 | tf_op jit(solution)/shard_map/ppermute | solution.py:308
  13.8 6.0 %collective-permute-start.6 = (bf16[224,256]{1,0:T(8,128)(2,1)S(1)}, bf16[224,256]{1,0:T(8,128)(2,1)S(1)}, u32[]{:S(2)}, u32[]{:S(2)}) collective-permute-start(bf16[224,256]{1,0:T(8,128)(2,1)S(1)} %pad_maximum_fusion.refs_0_), channel_id=1, source_target_pairs={{0,1},{1,0},{2,3},{3,2},{4,5},{5,4},{6,7},{7,6},{8,9},{9,8},{10,11... | collective-permute-start | bytes 344072 | tf_op jit(solution)/shard_map/ppermute | solution.py:308
  16.5 3.3 %collective-permute-start.9 = (bf16[224,256]{1,0:T(8,128)(2,1)S(1)}, bf16[224,256]{1,0:T(8,128)(2,1)S(1)}, u32[]{:S(2)}, u32[]{:S(2)}) collective-permute-start(bf16[224,256]{1,0:T(8,128)(2,1)S(1)} %collective-permute-done.5.refs_3_), channel_id=1, source_target_pairs={{0,1},{1,0},{2,3},{3,2},{4,5},{5,4},{6,7},{7,6},{8,9},{9,8},{10,11... | collective-permute-start | bytes 344072 | tf_op jit(solution)/shard_map/ppermute | solution.py:308
  19.3 1.3 %collective-permute-start.8 = (bf16[224,256]{1,0:T(8,128)(2,1)S(1)}, bf16[224,256]{1,0:T(8,128)(2,1)S(1)}, u32[]{:S(2)}, u32[]{:S(2)}) collective-permute-start(bf16[224,256]{1,0:T(8,128)(2,1)S(1)} %collective-permute-done.4.refs_2_), channel_id=1, source_target_pairs={{0,1},{1,0},{2,3},{3,2},{4,5},{5,4},{6,7},{7,6},{8,9},{9,8},{10,11... | collective-permute-start | bytes 344072 | tf_op jit(solution)/shard_map/ppermute | solution.py:308
  19.4 1.4 %collective-permute-start.7 = (bf16[224,256]{1,0:T(8,128)(2,1)S(1)}, bf16[224,256]{1,0:T(8,128)(2,1)S(1)}, u32[]{:S(2)}, u32[]{:S(2)}) collective-permute-start(bf16[224,256]{1,0:T(8,128)(2,1)S(1)} %collective-permute-done.3.refs_1_), channel_id=1, source_target_pairs={{0,1},{1,0},{2,3},{3,2},{4,5},{5,4},{6,7},{7,6},{8,9},{9,8},{10,11... | collective-permute-start | bytes 344072 | tf_op jit(solution)/shard_map/ppermute | solution.py:308

commit v4 on v3

--- a/solution.py
+++ b/solution.py
@@ -54,17 +54,19 @@
 
 def unpack(mesh_n, mol, owners, me, pieces, x_ref, pref_ref):
     rows_n, cols_n = mesh_n
-    seen = set()
-    for piece, masks in zip(pieces, owners):
+    tails = [None, None]
+    for i, (piece, masks) in enumerate(zip(pieces, owners)):
         for p, mask in enumerate(masks):
             owner = me ^ mask
             row, col = owner // cols_n, owner % cols_n
-            at = p * (mol + 8)
-            x_ref[pl.ds(pl.multiple_of((col * rows_n + row) * mol, 16), mol), :] = piece[at:at + mol, :]
-            if mask // cols_n not in seen:
-                seen.add(mask // cols_n)
-                tail = piece[at + mol:at + mol + 8, :].astype(F32)
-                pref_ref[pl.ds(row, 1), :] = (tail[0:1] + tail[1:2]) + tail[2:3]
+            x_ref[pl.ds(pl.multiple_of((col * rows_n + row) * mol, 16), mol), :] = piece[p * mol:(p + 1) * mol, :]
+        if i < len(pieces) // 2 and masks[0] % cols_n // 2 < 2:
+            flip = masks[0] // cols_n
+            tail = piece[len(masks) * mol:len(masks) * mol + 8, :].astype(F32)
+            tails[flip] = tail if tails[flip] is None else tails[flip] + tail
+    for flip, tail in enumerate(tails):
+        for far in range(rows_n // 2):
+            pref_ref[pl.ds(2 * far + (me // cols_n % 2 ^ flip), 1), :] = tail[2 * far:2 * far + 1] + tail[2 * far + 1:2 * far + 2]
 
 
 FIRST, GAIN, OWN, R1D, ONE, TWO, BASE, Z, R2D, AV1D, STAR, WZ = range(12)
@@ -273,9 +275,12 @@
         copy.wait()
     out_ref[0:mol, :] = e_ref[...]
     values = p_ref[...]
+    high, mid, low = thirds(values)
+    odd = lax.axis_index("col") // 2 % 2 == 1
     fill = jnp.zeros((1, out_ref.shape[1] - values.shape[1]), F32)
-    parts = [jnp.concatenate([part, fill], 1) for part in thirds(values)]
-    out_ref[mol:mol + 8, :] = jnp.concatenate(parts + [jnp.zeros((5, out_ref.shape[1]), F32)], 0).astype(BF16)
+    one, two = (jnp.concatenate([part, fill], 1) for part in (jnp.where(odd, low, high), jnp.where(odd, 0.0, mid)))
+    at = lax.broadcasted_iota(jnp.int32, (8, out_ref.shape[1]), 0) - lax.axis_index("row") // 2 * 2
+    out_ref[mol:mol + 8, :] = jnp.where(at == 0, one, jnp.where(at == 1, two, 0.0)).astype(BF16)
 
 
 def pack(embedding, preference):
@@ -292,7 +297,7 @@
 
 def fits(rows_n, cols_n, mol, width):
     n = mol * rows_n * cols_n
-    two = rows_n >= 2 and cols_n >= 2 and not rows_n & (rows_n - 1) and not cols_n & (cols_n - 1)
+    two = rows_n in (2, 4, 8) and cols_n >= 4 and not cols_n & (cols_n - 1)
     return (two and 4 * n * n <= 16 << 20 and n % 512 == 0 and mol * rows_n % LANES == 0 and mol % 16 == 0
             and mol * cols_n <= width and width % LANES == 0)
 
@@ -314,7 +319,8 @@
     rows, cols = mol * cols_n, mol * rows_n
     held = pack(embedding.reshape(mol, width), preference.reshape(1, rows))
     far, near = stages(rows_n, cols_n)
-    line = jnp.concatenate([held] + [swap(held, m) for m in far], 0)
+    line = [held] + [swap(held, m) for m in far]
+    line = jnp.concatenate([h[:mol] for h in line] + [sum(h[mol:] for h in line)], 0)
     pieces = [line] + [swap(line, m) for m in near]
     owners = [[n ^ f for f in [0] + far] for n in [0] + near]
     pieces = pieces + [swap(piece, 1) for piece in pieces]

time: 28.7 us -> 28.2 us (0.983)
  waiting for transfers between devices: 9.71 us -> 9.18 us
    ppermute x10, waiting for transfers between devices: 9.71 us -> 9.18 us  [swap(): lax.ppermute(block, ('row', 'col'), [(i, i ^ mask) for i in range(size)])]
where the time goes in v4:
time: 28.2 us; the launch traced here: 28 us
  starting transfers between devices  9.6 us (34%)
  waiting for transfers between devices  9.18 us (33%)
  Pallas kernels  8.53 us (30%)
  between operations  0.66 us (2%)
    ppermute x10, starting transfers between devices, swap(): lax.ppermute(block, ('row', 'col'), [(i, i ^ mask) for i in range(size)])  9.6 us
    ppermute x10, waiting for transfers between devices, swap(): lax.ppermute(block, ('row', 'col'), [(i, i ^ mask) for i in range(size)])  9.18 us
    pallas_call x1, Pallas kernels, compute(): pl.pallas_call(functools.partial(kernel, mesh_n, mol, owners, rows, cols,...  7.74 us
    pallas_call x1, Pallas kernels, pack(): pl.pallas_call(functools.partial(pack_kernel, mol), out_shape=pltpu.VMEM(...  0.8 us
  transfers between devices with their start and end apart: 10, of which 6 were waited for; matrix products, arithmetic and copies ran while one was open for 0% of the time, Pallas kernels for 0%

profile of v4, /device:TPU:0, one launch (start us, length us, event | category | flops | bytes accessed | tf_op | source)
XLA Modules:
  0.0 28.0 jit_solution(17542559358837074563)
XLA Ops:
  0.6 0.8 %shard_map.41 = bf16[56,256]{1,0:T(8,128)(2,1)S(1)} custom-call(bf16[48,256]{1,0:T(8,128)(2,1)} %bitcast.2, f32[1,192]{1,0:T(1,128)} %bitcast.3), custom_call_target="tpu_custom_call" | custom-call | tf_op jit(solution)/shard_map/pallas_call | solution.py:288
  1.4 4.6 %collective-permute-start.2 = (bf16[56,256]{1,0:T(8,128)(2,1)S(1)}, bf16[56,256]{1,0:T(8,128)(2,1)S(1)}, u32[]{:S(2)}, u32[]{:S(2)}) collective-permute-start(bf16[56,256]{1,0:T(8,128)(2,1)S(1)} %shard_map.41), channel_id=1, source_target_pairs={{0,25},{1,24},{2,27},{3,26},{4,29},{5,28},{6,31},{7,30},{8,17},{9,... | collective-permute-start | bytes 86024 | tf_op jit(solution)/shard_map/ppermute | solution.py:313
  6.0 0.0 collective-permute-start.1
  6.0 0.9 %collective-permute-start = (bf16[56,256]{1,0:T(8,128)(2,1)S(1)}, bf16[56,256]{1,0:T(8,128)(2,1)S(1)}, u32[]{:S(2)}, u32[]{:S(2)}) collective-permute-start(bf16[56,256]{1,0:T(8,128)(2,1)S(1)} %shard_map.41), channel_id=1, source_target_pairs={{0,9},{1,8},{2,11},{3,10},{4,13},{5,12},{6,15},{7,14},{8,1},{9,0},... | collective-permute-start | bytes 86024 | tf_op jit(solution)/shard_map/ppermute | solution.py:313
  6.9 2.4 %collective-permute-done = bf16[56,256]{1,0:T(8,128)(2,1)S(1)} collective-permute-done((bf16[56,256]{1,0:T(8,128)(2,1)S(1)}, bf16[56,256]{1,0:T(8,128)(2,1)S(1)}, u32[]{:S(2)}, u32[]{:S(2)}) %collective-permute-start) | collective-permute-done | bytes 28704 | tf_op jit(solution)/shard_map/ppermute | solution.py:313
  9.3 1.1 %collective-permute-done.1 = bf16[56,256]{1,0:T(8,128)(2,1)S(1)} collective-permute-done((bf16[56,256]{1,0:T(8,128)(2,1)S(1)}, bf16[56,256]{1,0:T(8,128)(2,1)S(1)}, u32[]{:S(2)}, u32[]{:S(2)}) %collective-permute-start.1) | collective-permute-done | bytes 28704 | tf_op jit(solution)/shard_map/ppermute | solution.py:313
  10.4 0.0 collective-permute-done.2
  10.5 2.6 %collective-permute-start.5 = (bf16[200,256]{1,0:T(8,128)(2,1)S(1)}, bf16[200,256]{1,0:T(8,128)(2,1)S(1)}, u32[]{:S(2)}, u32[]{:S(2)}) collective-permute-start(bf16[200,256]{1,0:T(8,128)(2,1)S(1)} %constant_dynamic-update-slice_fusion.refs_0_), channel_id=1, source_target_pairs={{0,7},{1,6},{2,5},{3,4},{4,3},{5,2},{6,1},{7,0},{8,15},{9,14},{10,... | collective-permute-start | bytes 307208 | tf_op jit(solution)/shard_map/ppermute | solution.py:313
  13.0 0.2 collective-permute-start.4
  13.2 0.6 %collective-permute-start.3 = (bf16[200,256]{1,0:T(8,128)(2,1)S(1)}, bf16[200,256]{1,0:T(8,128)(2,1)S(1)}, u32[]{:S(2)}, u32[]{:S(2)}) collective-permute-start(bf16[200,256]{1,0:T(8,128)(2,1)S(1)} %constant_dynamic-update-slice_fusion.refs_0_), channel_id=1, source_target_pairs={{0,3},{1,2},{2,1},{3,0},{4,7},{5,6},{6,5},{7,4},{8,11},{9,10},{10,... | collective-permute-start | bytes 307208 | tf_op jit(solution)/shard_map/ppermute | solution.py:313
  13.8 0.1 collective-permute-start.6
  13.9 2.4 %collective-permute-done.5.refs_3_ = bf16[200,256]{1,0:T(8,128)(2,1)S(1)} collective-permute-done((bf16[200,256]{1,0:T(8,128)(2,1)S(1)}, bf16[200,256]{1,0:T(8,128)(2,1)S(1)}, u32[]{:S(2)}, u32[]{:S(2)}) %collective-permute-start.5) | collective-permute-done | bytes 102432 | tf_op jit(solution)/shard_map/ppermute | solution.py:313
  16.3 0.2 collective-permute-start.9
  16.5 2.3 %collective-permute-done.4.refs_2_ = bf16[200,256]{1,0:T(8,128)(2,1)S(1)} collective-permute-done((bf16[200,256]{1,0:T(8,128)(2,1)S(1)}, bf16[200,256]{1,0:T(8,128)(2,1)S(1)}, u32[]{:S(2)}, u32[]{:S(2)}) %collective-permute-start.4) | collective-permute-done | bytes 102432 | tf_op jit(solution)/shard_map/ppermute | solution.py:313
  18.8 0.1 collective-permute-start.8
  18.9 0.0 collective-permute-done.3.refs_1_
  18.9 0.4 %collective-permute-start.7 = (bf16[200,256]{1,0:T(8,128)(2,1)S(1)}, bf16[200,256]{1,0:T(8,128)(2,1)S(1)}, u32[]{:S(2)}, u32[]{:S(2)}) collective-permute-start(bf16[200,256]{1,0:T(8,128)(2,1)S(1)} %collective-permute-done.3.refs_1_), channel_id=1, source_target_pairs={{0,1},{1,0},{2,3},{3,2},{4,5},{5,4},{6,7},{7,6},{8,9},{9,8},{10,11... | collective-permute-start | bytes 307208 | tf_op jit(solution)/shard_map/ppermute | solution.py:313
  19.3 0.0 collective-permute-done.6.refs_4_
  19.3 0.0 collective-permute-done.9.refs_7_
  19.3 0.8 %collective-permute-done.8.refs_6_ = bf16[200,256]{1,0:T(8,128)(2,1)S(1)} collective-permute-done((bf16[200,256]{1,0:T(8,128)(2,1)S(1)}, bf16[200,256]{1,0:T(8,128)(2,1)S(1)}, u32[]{:S(2)}, u32[]{:S(2)}) %collective-permute-start.8) | collective-permute-done | bytes 102432 | tf_op jit(solution)/shard_map/ppermute | solution.py:313
  20.1 0.2 collective-permute-done.7.refs_5_
  20.3 7.7 %shard_map.42 = (f32[192,384]{1,0:T(8,128)}, f32[192,384]{1,0:T(8,128)}) custom-call(bf16[200,256]{1,0:T(8,128)(2,1)S(1)} %constant_dynamic-update-slice_fusion.refs_0_, bf16[200,256]{1,0:T(8,128)(2,1)S(1)} %collective-permute-done.3.refs_1_, bf16[200,256]{1,0:T(8,128)(2,1)S(1)} %collective-permute-done.4.refs_2_, ...), custom_call_target="tpu_custom_call" | custom-call | tf_op jit(solution)/shard_map/pallas_call | solution.py:244
  (5 shorter events, 0.0 us)
Async XLA Ops:
  1.4 9.0 %collective-permute-start.2 = (bf16[56,256]{1,0:T(8,128)(2,1)S(1)}, bf16[56,256]{1,0:T(8,128)(2,1)S(1)}, u32[]{:S(2)}, u32[]{:S(2)}) collective-permute-start(bf16[56,256]{1,0:T(8,128)(2,1)S(1)} %shard_map.41), channel_id=1, source_target_pairs={{0,25},{1,24},{2,27},{3,26},{4,29},{5,28},{6,31},{7,30},{8,17},{9,... | collective-permute-start | bytes 86024 | tf_op jit(solution)/shard_map/ppermute | solution.py:313
  6.0 4.5 %collective-permute-start.1 = (bf16[56,256]{1,0:T(8,128)(2,1)S(1)}, bf16[56,256]{1,0:T(8,128)(2,1)S(1)}, u32[]{:S(2)}, u32[]{:S(2)}) collective-permute-start(bf16[56,256]{1,0:T(8,128)(2,1)S(1)} %shard_map.41), channel_id=1, source_target_pairs={{0,17},{1,16},{2,19},{3,18},{4,21},{5,20},{6,23},{7,22},{8,25},{9,... | collective-permute-start | bytes 86024 | tf_op jit(solution)/shard_map/ppermute | solution.py:313
  6.0 3.3 %collective-permute-start = (bf16[56,256]{1,0:T(8,128)(2,1)S(1)}, bf16[56,256]{1,0:T(8,128)(2,1)S(1)}, u32[]{:S(2)}, u32[]{:S(2)}) collective-permute-start(bf16[56,256]{1,0:T(8,128)(2,1)S(1)} %shard_map.41), channel_id=1, source_target_pairs={{0,9},{1,8},{2,11},{3,10},{4,13},{5,12},{6,15},{7,14},{8,1},{9,0},... | collective-permute-start | bytes 86024 | tf_op jit(solution)/shard_map/ppermute | solution.py:313
  10.5 5.8 %collective-permute-start.5 = (bf16[200,256]{1,0:T(8,128)(2,1)S(1)}, bf16[200,256]{1,0:T(8,128)(2,1)S(1)}, u32[]{:S(2)}, u32[]{:S(2)}) collective-permute-start(bf16[200,256]{1,0:T(8,128)(2,1)S(1)} %constant_dynamic-update-slice_fusion.refs_0_), channel_id=1, source_target_pairs={{0,7},{1,6},{2,5},{3,4},{4,3},{5,2},{6,1},{7,0},{8,15},{9,14},{10,... | collective-permute-start | bytes 307208 | tf_op jit(solution)/shard_map/ppermute | solution.py:313
  13.0 5.8 %collective-permute-start.4 = (bf16[200,256]{1,0:T(8,128)(2,1)S(1)}, bf16[200,256]{1,0:T(8,128)(2,1)S(1)}, u32[]{:S(2)}, u32[]{:S(2)}) collective-permute-start(bf16[200,256]{1,0:T(8,128)(2,1)S(1)} %constant_dynamic-update-slice_fusion.refs_0_), channel_id=1, source_target_pairs={{0,5},{1,4},{2,7},{3,6},{4,1},{5,0},{6,3},{7,2},{8,13},{9,12},{10,... | collective-permute-start | bytes 307208 | tf_op jit(solution)/shard_map/ppermute | solution.py:313
  13.2 5.7 %collective-permute-start.3 = (bf16[200,256]{1,0:T(8,128)(2,1)S(1)}, bf16[200,256]{1,0:T(8,128)(2,1)S(1)}, u32[]{:S(2)}, u32[]{:S(2)}) collective-permute-start(bf16[200,256]{1,0:T(8,128)(2,1)S(1)} %constant_dynamic-update-slice_fusion.refs_0_), channel_id=1, source_target_pairs={{0,3},{1,2},{2,1},{3,0},{4,7},{5,6},{6,5},{7,4},{8,11},{9,10},{10,... | collective-permute-start | bytes 307208 | tf_op jit(solution)/shard_map/ppermute | solution.py:313
  13.8 5.5 %collective-permute-start.6 = (bf16[200,256]{1,0:T(8,128)(2,1)S(1)}, bf16[200,256]{1,0:T(8,128)(2,1)S(1)}, u32[]{:S(2)}, u32[]{:S(2)}) collective-permute-start(bf16[200,256]{1,0:T(8,128)(2,1)S(1)} %constant_dynamic-update-slice_fusion.refs_0_), channel_id=1, source_target_pairs={{0,1},{1,0},{2,3},{3,2},{4,5},{5,4},{6,7},{7,6},{8,9},{9,8},{10,11... | collective-permute-start | bytes 307208 | tf_op jit(solution)/shard_map/ppermute | solution.py:313
  16.3 3.0 %collective-permute-start.9 = (bf16[200,256]{1,0:T(8,128)(2,1)S(1)}, bf16[200,256]{1,0:T(8,128)(2,1)S(1)}, u32[]{:S(2)}, u32[]{:S(2)}) collective-permute-start(bf16[200,256]{1,0:T(8,128)(2,1)S(1)} %collective-permute-done.5.refs_3_), channel_id=1, source_target_pairs={{0,1},{1,0},{2,3},{3,2},{4,5},{5,4},{6,7},{7,6},{8,9},{9,8},{10,11... | collective-permute-start | bytes 307208 | tf_op jit(solution)/shard_map/ppermute | solution.py:313
  18.8 1.3 %collective-permute-start.8 = (bf16[200,256]{1,0:T(8,128)(2,1)S(1)}, bf16[200,256]{1,0:T(8,128)(2,1)S(1)}, u32[]{:S(2)}, u32[]{:S(2)}) collective-permute-start(bf16[200,256]{1,0:T(8,128)(2,1)S(1)} %collective-permute-done.4.refs_2_), channel_id=1, source_target_pairs={{0,1},{1,0},{2,3},{3,2},{4,5},{5,4},{6,7},{7,6},{8,9},{9,8},{10,11... | collective-permute-start | bytes 307208 | tf_op jit(solution)/shard_map/ppermute | solution.py:313
  18.9 1.3 %collective-permute-start.7 = (bf16[200,256]{1,0:T(8,128)(2,1)S(1)}, bf16[200,256]{1,0:T(8,128)(2,1)S(1)}, u32[]{:S(2)}, u32[]{:S(2)}) collective-permute-start(bf16[200,256]{1,0:T(8,128)(2,1)S(1)} %collective-permute-done.3.refs_1_), channel_id=1, source_target_pairs={{0,1},{1,0},{2,3},{3,2},{4,5},{5,4},{6,7},{7,6},{8,9},{9,8},{10,11... | collective-permute-start | bytes 307208 | tf_op jit(solution)/shard_map/ppermute | solution.py:313

commit v5 on v4

--- a/solution.py
+++ b/solution.py
@@ -41,25 +41,31 @@
     return high, mid, rest - mid
 
 
-def squares(x_ref, q_ref, step):
-    n, width = x_ref.shape
-    ones = jnp.ones((2 * width, LANES), BF16)
-    for s in range(0, n, step):
-        x = x_ref[s:s + step, :].astype(F32)
-        x = x * x
-        high = x.astype(BF16)
-        low = (x - high.astype(F32)).astype(BF16)
-        q_ref[s:s + step, :] = jnp.dot(jnp.concatenate([high, low], 1), ones, preferred_element_type=F32)
-
-
-def unpack(mesh_n, mol, owners, me, pieces, x_ref, pref_ref):
+def squares(x):
+    ones = jnp.ones((2 * x.shape[1], LANES), BF16)
+    x = x.astype(F32)
+    x = x * x
+    high = x.astype(BF16)
+    low = (x - high.astype(F32)).astype(BF16)
+    return jnp.dot(jnp.concatenate([high, low], 1), ones, preferred_element_type=F32)
+
+
+def unpack(mesh_n, mol, owners, me, pieces, early, early_ref, x_ref, q_ref, pref_ref):
     rows_n, cols_n = mesh_n
     tails = [None, None]
     for i, (piece, masks) in enumerate(zip(pieces, owners)):
+        if i not in early:
+            q = squares(piece[0:len(masks) * mol, :])
         for p, mask in enumerate(masks):
             owner = me ^ mask
             row, col = owner // cols_n, owner % cols_n
-            x_ref[pl.ds(pl.multiple_of((col * rows_n + row) * mol, 16), mol), :] = piece[p * mol:(p + 1) * mol, :]
+            at = pl.ds(pl.multiple_of((col * rows_n + row) * mol, 16), mol)
+            x_ref[at, :] = piece[p * mol:(p + 1) * mol, :]
+            if i in early:
+                start = (early.index(i) * len(masks) + p) * mol
+                q_ref[at, :] = early_ref[start:start + mol, :]
+            else:
+                q_ref[at, :] = q[p * mol:(p + 1) * mol, :]
         if i < len(pieces) // 2 and masks[0] % cols_n // 2 < 2:
             flip = masks[0] // cols_n
             tail = piece[len(masks) * mol:len(masks) * mol + 8, :].astype(F32)
@@ -72,14 +78,13 @@
 FIRST, GAIN, OWN, R1D, ONE, TWO, BASE, Z, R2D, AV1D, STAR, WZ = range(12)
 
 
-def kernel(mesh_n, mol, owners, rows, cols, win, *refs, T=512, R=256, QS=256):
-    pieces, refs = refs[:len(owners)], refs[len(owners):]
+def kernel(mesh_n, mol, owners, early, rows, cols, win, *refs, T=512, R=256):
+    early_ref, pieces, refs = refs[0], refs[1:len(owners) + 1], refs[len(owners) + 1:]
     resp_ref, avail_ref, x_ref, pref_ref, g_ref, c_ref, a_ref, q_ref, row_ref, k_ref, r_out, a_out, t_ref, out_sem = refs
     n, width = x_ref.shape
     rows_n, cols_n = mesh_n
     row_idx, col_idx = lax.axis_index("row"), lax.axis_index("col")
-    unpack(mesh_n, mol, owners, row_idx * cols_n + col_idx, pieces, x_ref, pref_ref)
-    squares(x_ref, q_ref, QS)
+    unpack(mesh_n, mol, owners, row_idx * cols_n + col_idx, pieces, early, early_ref, x_ref, q_ref, pref_ref)
     sub8 = lax.broadcasted_iota(jnp.int32, (8, LANES), 0)
     lane8 = lax.broadcasted_iota(jnp.int32, (8, LANES), 1)
     gap = lane8 - sub8
@@ -238,13 +243,27 @@
         copy.wait()
 
 
-def compute(pieces, mesh_n, mol, owners, rows, cols):
+def squares_kernel(count, *refs):
+    for i, piece in enumerate(refs[:-1]):
+        refs[-1][i * count:(i + 1) * count, :] = squares(piece[0:count, :])
+
+
+def compute(pieces, mesh_n, mol, owners, early, rows, cols):
     n, width = mol * mesh_n[0] * mesh_n[1], pieces[0].shape[1]
     win = -(-(rows + LANES - math.gcd(rows, LANES)) // LANES) * LANES
+    count = len(owners[0]) * mol
+    sums = pl.pallas_call(
+        functools.partial(squares_kernel, count),
+        out_shape=jax.ShapeDtypeStruct((len(early) * count, LANES), F32),
+        in_specs=[pl.BlockSpec(memory_space=pltpu.VMEM)] * len(early),
+        out_specs=pl.BlockSpec(memory_space=pltpu.VMEM),
+        cost_estimate=pl.CostEstimate(flops=len(early) * count * 4 * width * LANES, bytes_accessed=4 << 20, transcendentals=0),
+        compiler_params=pltpu.CompilerParams(vmem_limit_bytes=40 << 20),
+    )(*[pieces[i] for i in early])
     return pl.pallas_call(
-        functools.partial(kernel, mesh_n, mol, owners, rows, cols, win),
+        functools.partial(kernel, mesh_n, mol, owners, early, rows, cols, win),
         out_shape=[jax.ShapeDtypeStruct((rows, cols), F32)] * 2,
-        in_specs=[pl.BlockSpec(memory_space=pltpu.VMEM)] * len(pieces),
+        in_specs=[pl.BlockSpec(memory_space=pltpu.VMEM)] * (len(pieces) + 1),
         out_specs=[pl.BlockSpec(memory_space=pl.ANY)] * 2,
         scratch_shapes=[
             pltpu.VMEM((n, width), BF16),
@@ -261,7 +280,7 @@
             pltpu.SemaphoreType.DMA((cols // LANES, 2)),
         ],
         compiler_params=pltpu.CompilerParams(vmem_limit_bytes=40 << 20),
-    )(*pieces)
+    )(sums, *pieces)
 
 
 def pack_kernel(mol, embedding_ref, preference_ref, out_ref, e_ref, p_ref, sems):
@@ -325,7 +344,8 @@
     owners = [[n ^ f for f in [0] + far] for n in [0] + near]
     pieces = pieces + [swap(piece, 1) for piece in pieces]
     owners = owners + [[m ^ 1 for m in masks] for masks in owners]
-    return tuple(compute(pieces, (rows_n, cols_n), mol, owners, rows, cols))
+    early = (*range(len(near) + 2), 2 * len(near) + 1)
+    return tuple(compute(pieces, (rows_n, cols_n), mol, owners, early, rows, cols))
 
 
 def local(embedding, preference):

time: 28.2 us -> 27.9 us (0.989)
  waiting for transfers between devices: 9.18 us -> 8.71 us
    ppermute x10, waiting for transfers between devices: 9.18 us -> 8.71 us  [swap(): lax.ppermute(block, ('row', 'col'), [(i, i ^ mask) for i in range(size)])]
    pallas_call x1 -> x2, Pallas kernels: 7.74 us -> 7.94 us  [the longest x1 7.48 us: compute(): pl.pallas_call(functools.partial(kernel, mesh_n, mol, owners, early, rows...]
  transfers between devices with their start and end apart: 10 -> 10, of which waited for: 6 -> 6; matrix products, arithmetic and copies ran while one was open for 0% -> 0% of each run, Pallas kernels for 0% -> 2%
where the time goes in v5:
time: 27.9 us; the launch traced here: 27.7 us
  starting transfers between devices  9.6 us (34%)
  Pallas kernels  8.74 us (31%)
  waiting for transfers between devices  8.71 us (31%)
  between operations  0.66 us (2%)
    ppermute x10, starting transfers between devices, swap(): lax.ppermute(block, ('row', 'col'), [(i, i ^ mask) for i in range(size)])  9.6 us
    ppermute x10, waiting for transfers between devices, swap(): lax.ppermute(block, ('row', 'col'), [(i, i ^ mask) for i in range(size)])  8.71 us
    pallas_call x1, Pallas kernels, compute(): pl.pallas_call(functools.partial(kernel, mesh_n, mol, owners, early, rows...  7.48 us
    pallas_call x1, Pallas kernels, pack(): pl.pallas_call(functools.partial(pack_kernel, mol), out_shape=pltpu.VMEM(...  0.8 us
  transfers between devices with their start and end apart: 10, of which 6 were waited for; matrix products, arithmetic and copies ran while one was open for 0% of the time, Pallas kernels for 2%

profile of v5, /device:TPU:0, one launch (start us, length us, event | category | flops | bytes accessed | tf_op | source)
XLA Modules:
  0.0 27.7 jit_solution(4671712643806943307)
XLA Ops:
  0.6 0.8 %shard_map.41 = bf16[56,256]{1,0:T(8,128)(2,1)S(1)} custom-call(bf16[48,256]{1,0:T(8,128)(2,1)} %bitcast.2, f32[1,192]{1,0:T(1,128)} %bitcast.3), custom_call_target="tpu_custom_call" | custom-call | tf_op jit(solution)/shard_map/pallas_call | solution.py:307
  1.4 4.6 %collective-permute-start.2 = (bf16[56,256]{1,0:T(8,128)(2,1)S(1)}, bf16[56,256]{1,0:T(8,128)(2,1)S(1)}, u32[]{:S(2)}, u32[]{:S(2)}) collective-permute-start(bf16[56,256]{1,0:T(8,128)(2,1)S(1)} %shard_map.41), channel_id=1, source_target_pairs={{0,25},{1,24},{2,27},{3,26},{4,29},{5,28},{6,31},{7,30},{8,17},{9,... | collective-permute-start | bytes 86024 | tf_op jit(solution)/shard_map/ppermute | solution.py:332
  6.0 0.0 collective-permute-start.1
  6.0 0.9 %collective-permute-start = (bf16[56,256]{1,0:T(8,128)(2,1)S(1)}, bf16[56,256]{1,0:T(8,128)(2,1)S(1)}, u32[]{:S(2)}, u32[]{:S(2)}) collective-permute-start(bf16[56,256]{1,0:T(8,128)(2,1)S(1)} %shard_map.41), channel_id=1, source_target_pairs={{0,9},{1,8},{2,11},{3,10},{4,13},{5,12},{6,15},{7,14},{8,1},{9,0},... | collective-permute-start | bytes 86024 | tf_op jit(solution)/shard_map/ppermute | solution.py:332
  6.9 2.4 %collective-permute-done = bf16[56,256]{1,0:T(8,128)(2,1)S(1)} collective-permute-done((bf16[56,256]{1,0:T(8,128)(2,1)S(1)}, bf16[56,256]{1,0:T(8,128)(2,1)S(1)}, u32[]{:S(2)}, u32[]{:S(2)}) %collective-permute-start) | collective-permute-done | bytes 28704 | tf_op jit(solution)/shard_map/ppermute | solution.py:332
  9.3 1.1 %collective-permute-done.1 = bf16[56,256]{1,0:T(8,128)(2,1)S(1)} collective-permute-done((bf16[56,256]{1,0:T(8,128)(2,1)S(1)}, bf16[56,256]{1,0:T(8,128)(2,1)S(1)}, u32[]{:S(2)}, u32[]{:S(2)}) %collective-permute-start.1) | collective-permute-done | bytes 28704 | tf_op jit(solution)/shard_map/ppermute | solution.py:332
  10.4 0.0 collective-permute-done.2
  10.5 2.6 %collective-permute-start.5 = (bf16[200,256]{1,0:T(8,128)(2,1)S(1)}, bf16[200,256]{1,0:T(8,128)(2,1)S(1)}, u32[]{:S(2)}, u32[]{:S(2)}) collective-permute-start(bf16[200,256]{1,0:T(8,128)(2,1)S(1)} %constant_dynamic-update-slice_fusion.refs_0_.refs_1_), channel_id=1, source_target_pairs={{0,7},{1,6},{2,5},{3,4},{4,3},{5,2},{6,1},{7,0},{8,15},{9,14},{10,... | collective-permute-start | bytes 307208 | tf_op jit(solution)/shard_map/ppermute | solution.py:332
  13.0 0.2 collective-permute-start.4
  13.2 0.6 %collective-permute-start.3 = (bf16[200,256]{1,0:T(8,128)(2,1)S(1)}, bf16[200,256]{1,0:T(8,128)(2,1)S(1)}, u32[]{:S(2)}, u32[]{:S(2)}) collective-permute-start(bf16[200,256]{1,0:T(8,128)(2,1)S(1)} %constant_dynamic-update-slice_fusion.refs_0_.refs_1_), channel_id=1, source_target_pairs={{0,3},{1,2},{2,1},{3,0},{4,7},{5,6},{6,5},{7,4},{8,11},{9,10},{10,... | collective-permute-start | bytes 307208 | tf_op jit(solution)/shard_map/ppermute | solution.py:332
  13.8 0.1 collective-permute-start.6
  13.9 2.4 %collective-permute-done.5.refs_3_.refs_4_ = bf16[200,256]{1,0:T(8,128)(2,1)S(1)} collective-permute-done((bf16[200,256]{1,0:T(8,128)(2,1)S(1)}, bf16[200,256]{1,0:T(8,128)(2,1)S(1)}, u32[]{:S(2)}, u32[]{:S(2)}) %collective-permute-start.5) | collective-permute-done | bytes 102432 | tf_op jit(solution)/shard_map/ppermute | solution.py:332
  16.3 0.2 collective-permute-start.7
  16.5 2.3 %collective-permute-done.4.refs_2_.refs_3_ = bf16[200,256]{1,0:T(8,128)(2,1)S(1)} collective-permute-done((bf16[200,256]{1,0:T(8,128)(2,1)S(1)}, bf16[200,256]{1,0:T(8,128)(2,1)S(1)}, u32[]{:S(2)}, u32[]{:S(2)}) %collective-permute-start.4) | collective-permute-done | bytes 102432 | tf_op jit(solution)/shard_map/ppermute | solution.py:332
  18.8 0.1 collective-permute-start.9
  18.9 0.0 collective-permute-done.3.refs_1_.refs_2_
  18.9 0.4 %collective-permute-start.8 = (bf16[200,256]{1,0:T(8,128)(2,1)S(1)}, bf16[200,256]{1,0:T(8,128)(2,1)S(1)}, u32[]{:S(2)}, u32[]{:S(2)}) collective-permute-start(bf16[200,256]{1,0:T(8,128)(2,1)S(1)} %collective-permute-done.3.refs_1_.refs_2_), channel_id=1, source_target_pairs={{0,1},{1,0},{2,3},{3,2},{4,5},{5,4},{6,7},{7,6},{8,9},{9,8},{10,11... | collective-permute-start | bytes 307208 | tf_op jit(solution)/shard_map/ppermute | solution.py:332
  19.3 0.0 collective-permute-done.6.refs_4_.refs_5_
  19.3 0.0 collective-permute-done.7.refs_5_.refs_8_
  19.3 0.5 %shard_map.42.refs_0_ = f32[1152,128]{1,0:T(8,128)S(1)} custom-call(bf16[200,256]{1,0:T(8,128)(2,1)S(1)} %constant_dynamic-update-slice_fusion.refs_0_.refs_1_, bf16[200,256]{1,0:T(8,128)(2,1)S(1)} %collective-permute-done.3.refs_1_.refs_2_, bf16[200,256]{1,0:T(8,128)(2,1)S(1)} %collective-permute-done.4.refs_2_.refs_3_, ...), custom_call_target="tpu_custom_call" | custom-call | flops 150994944 | bytes 4194304 | tf_op jit(solution)/shard_map/pallas_call | solution.py:255
  19.8 0.3 %collective-permute-done.9.refs_7_ = bf16[200,256]{1,0:T(8,128)(2,1)S(1)} collective-permute-done((bf16[200,256]{1,0:T(8,128)(2,1)S(1)}, bf16[200,256]{1,0:T(8,128)(2,1)S(1)}, u32[]{:S(2)}, u32[]{:S(2)}) %collective-permute-start.9) | collective-permute-done | bytes 102432 | tf_op jit(solution)/shard_map/ppermute | solution.py:332
  20.1 0.2 collective-permute-done.8.refs_6_
  20.3 7.5 %shard_map.43 = (f32[192,384]{1,0:T(8,128)}, f32[192,384]{1,0:T(8,128)}) custom-call(f32[1152,128]{1,0:T(8,128)S(1)} %shard_map.42.refs_0_, bf16[200,256]{1,0:T(8,128)(2,1)S(1)} %constant_dynamic-update-slice_fusion.refs_0_.refs_1_, bf16[200,256]{1,0:T(8,128)(2,1)S(1)} %collective-permute-done.3.refs_1_.refs_2_, ...), custom_call_target="tpu_custom_call" | custom-call | tf_op jit(solution)/shard_map/pallas_call | solution.py:263
  (5 shorter events, 0.0 us)
Async XLA Ops:
  1.4 9.0 %collective-permute-start.2 = (bf16[56,256]{1,0:T(8,128)(2,1)S(1)}, bf16[56,256]{1,0:T(8,128)(2,1)S(1)}, u32[]{:S(2)}, u32[]{:S(2)}) collective-permute-start(bf16[56,256]{1,0:T(8,128)(2,1)S(1)} %shard_map.41), channel_id=1, source_target_pairs={{0,25},{1,24},{2,27},{3,26},{4,29},{5,28},{6,31},{7,30},{8,17},{9,... | collective-permute-start | bytes 86024 | tf_op jit(solution)/shard_map/ppermute | solution.py:332
  6.0 4.5 %collective-permute-start.1 = (bf16[56,256]{1,0:T(8,128)(2,1)S(1)}, bf16[56,256]{1,0:T(8,128)(2,1)S(1)}, u32[]{:S(2)}, u32[]{:S(2)}) collective-permute-start(bf16[56,256]{1,0:T(8,128)(2,1)S(1)} %shard_map.41), channel_id=1, source_target_pairs={{0,17},{1,16},{2,19},{3,18},{4,21},{5,20},{6,23},{7,22},{8,25},{9,... | collective-permute-start | bytes 86024 | tf_op jit(solution)/shard_map/ppermute | solution.py:332
  6.0 3.3 %collective-permute-start = (bf16[56,256]{1,0:T(8,128)(2,1)S(1)}, bf16[56,256]{1,0:T(8,128)(2,1)S(1)}, u32[]{:S(2)}, u32[]{:S(2)}) collective-permute-start(bf16[56,256]{1,0:T(8,128)(2,1)S(1)} %shard_map.41), channel_id=1, source_target_pairs={{0,9},{1,8},{2,11},{3,10},{4,13},{5,12},{6,15},{7,14},{8,1},{9,0},... | collective-permute-start | bytes 86024 | tf_op jit(solution)/shard_map/ppermute | solution.py:332
  10.5 5.8 %collective-permute-start.5 = (bf16[200,256]{1,0:T(8,128)(2,1)S(1)}, bf16[200,256]{1,0:T(8,128)(2,1)S(1)}, u32[]{:S(2)}, u32[]{:S(2)}) collective-permute-start(bf16[200,256]{1,0:T(8,128)(2,1)S(1)} %constant_dynamic-update-slice_fusion.refs_0_.refs_1_), channel_id=1, source_target_pairs={{0,7},{1,6},{2,5},{3,4},{4,3},{5,2},{6,1},{7,0},{8,15},{9,14},{10,... | collective-permute-start | bytes 307208 | tf_op jit(solution)/shard_map/ppermute | solution.py:332
  13.0 5.8 %collective-permute-start.4 = (bf16[200,256]{1,0:T(8,128)(2,1)S(1)}, bf16[200,256]{1,0:T(8,128)(2,1)S(1)}, u32[]{:S(2)}, u32[]{:S(2)}) collective-permute-start(bf16[200,256]{1,0:T(8,128)(2,1)S(1)} %constant_dynamic-update-slice_fusion.refs_0_.refs_1_), channel_id=1, source_target_pairs={{0,5},{1,4},{2,7},{3,6},{4,1},{5,0},{6,3},{7,2},{8,13},{9,12},{10,... | collective-permute-start | bytes 307208 | tf_op jit(solution)/shard_map/ppermute | solution.py:332
  13.2 5.7 %collective-permute-start.3 = (bf16[200,256]{1,0:T(8,128)(2,1)S(1)}, bf16[200,256]{1,0:T(8,128)(2,1)S(1)}, u32[]{:S(2)}, u32[]{:S(2)}) collective-permute-start(bf16[200,256]{1,0:T(8,128)(2,1)S(1)} %constant_dynamic-update-slice_fusion.refs_0_.refs_1_), channel_id=1, source_target_pairs={{0,3},{1,2},{2,1},{3,0},{4,7},{5,6},{6,5},{7,4},{8,11},{9,10},{10,... | collective-permute-start | bytes 307208 | tf_op jit(solution)/shard_map/ppermute | solution.py:332
  13.8 5.5 %collective-permute-start.6 = (bf16[200,256]{1,0:T(8,128)(2,1)S(1)}, bf16[200,256]{1,0:T(8,128)(2,1)S(1)}, u32[]{:S(2)}, u32[]{:S(2)}) collective-permute-start(bf16[200,256]{1,0:T(8,128)(2,1)S(1)} %constant_dynamic-update-slice_fusion.refs_0_.refs_1_), channel_id=1, source_target_pairs={{0,1},{1,0},{2,3},{3,2},{4,5},{5,4},{6,7},{7,6},{8,9},{9,8},{10,11... | collective-permute-start | bytes 307208 | tf_op jit(solution)/shard_map/ppermute | solution.py:332
  16.3 3.0 %collective-permute-start.7 = (bf16[200,256]{1,0:T(8,128)(2,1)S(1)}, bf16[200,256]{1,0:T(8,128)(2,1)S(1)}, u32[]{:S(2)}, u32[]{:S(2)}) collective-permute-start(bf16[200,256]{1,0:T(8,128)(2,1)S(1)} %collective-permute-done.5.refs_3_.refs_4_), channel_id=1, source_target_pairs={{0,1},{1,0},{2,3},{3,2},{4,5},{5,4},{6,7},{7,6},{8,9},{9,8},{10,11... | collective-permute-start | bytes 307208 | tf_op jit(solution)/shard_map/ppermute | solution.py:332
  18.8 1.3 %collective-permute-start.9 = (bf16[200,256]{1,0:T(8,128)(2,1)S(1)}, bf16[200,256]{1,0:T(8,128)(2,1)S(1)}, u32[]{:S(2)}, u32[]{:S(2)}) collective-permute-start(bf16[200,256]{1,0:T(8,128)(2,1)S(1)} %collective-permute-done.4.refs_2_.refs_3_), channel_id=1, source_target_pairs={{0,1},{1,0},{2,3},{3,2},{4,5},{5,4},{6,7},{7,6},{8,9},{9,8},{10,11... | collective-permute-start | bytes 307208 | tf_op jit(solution)/shard_map/ppermute | solution.py:332
  18.9 1.3 %collective-permute-start.8 = (bf16[200,256]{1,0:T(8,128)(2,1)S(1)}, bf16[200,256]{1,0:T(8,128)(2,1)S(1)}, u32[]{:S(2)}, u32[]{:S(2)}) collective-permute-start(bf16[200,256]{1,0:T(8,128)(2,1)S(1)} %collective-permute-done.3.refs_1_.refs_2_), channel_id=1, source_target_pairs={{0,1},{1,0},{2,3},{3,2},{4,5},{5,4},{6,7},{7,6},{8,9},{9,8},{10,11... | collective-permute-start | bytes 307208 | tf_op jit(solution)/shard_map/ppermute | solution.py:332

commit v6 on v5

--- a/solution.py
+++ b/solution.py
@@ -50,22 +50,23 @@
     return jnp.dot(jnp.concatenate([high, low], 1), ones, preferred_element_type=F32)
 
 
-def unpack(mesh_n, mol, owners, me, pieces, early, early_ref, x_ref, q_ref, pref_ref):
+def place(mesh_n, mol, me, piece, masks, x_ref, q_ref):
+    rows_n, cols_n = mesh_n
+    q = squares(piece[0:len(masks) * mol, :])
+    for p, mask in enumerate(masks):
+        owner = me ^ mask
+        row, col = owner // cols_n, owner % cols_n
+        at = pl.ds(pl.multiple_of((col * rows_n + row) * mol, 16), mol)
+        x_ref[at, :] = piece[p * mol:(p + 1) * mol, :]
+        q_ref[at, :] = q[p * mol:(p + 1) * mol, :]
+
+
+def unpack(mesh_n, mol, owners, me, pieces, early, x_ref, q_ref, pref_ref):
     rows_n, cols_n = mesh_n
     tails = [None, None]
     for i, (piece, masks) in enumerate(zip(pieces, owners)):
         if i not in early:
-            q = squares(piece[0:len(masks) * mol, :])
-        for p, mask in enumerate(masks):
-            owner = me ^ mask
-            row, col = owner // cols_n, owner % cols_n
-            at = pl.ds(pl.multiple_of((col * rows_n + row) * mol, 16), mol)
-            x_ref[at, :] = piece[p * mol:(p + 1) * mol, :]
-            if i in early:
-                start = (early.index(i) * len(masks) + p) * mol
-                q_ref[at, :] = early_ref[start:start + mol, :]
-            else:
-                q_ref[at, :] = q[p * mol:(p + 1) * mol, :]
+            place(mesh_n, mol, me, piece, masks, x_ref, q_ref)
         if i < len(pieces) // 2 and masks[0] % cols_n // 2 < 2:
             flip = masks[0] // cols_n
             tail = piece[len(masks) * mol:len(masks) * mol + 8, :].astype(F32)
@@ -79,12 +80,12 @@
 
 
 def kernel(mesh_n, mol, owners, early, rows, cols, win, *refs, T=512, R=256):
-    early_ref, pieces, refs = refs[0], refs[1:len(owners) + 1], refs[len(owners) + 1:]
-    resp_ref, avail_ref, x_ref, pref_ref, g_ref, c_ref, a_ref, q_ref, row_ref, k_ref, r_out, a_out, t_ref, out_sem = refs
+    pieces, refs = refs[2:len(owners) + 2], refs[len(owners) + 2:]
+    resp_ref, avail_ref, x_ref, q_ref, pref_ref, g_ref, c_ref, a_ref, row_ref, k_ref, r_out, a_out, t_ref, out_sem = refs
     n, width = x_ref.shape
     rows_n, cols_n = mesh_n
     row_idx, col_idx = lax.axis_index("row"), lax.axis_index("col")
-    unpack(mesh_n, mol, owners, row_idx * cols_n + col_idx, pieces, early, early_ref, x_ref, q_ref, pref_ref)
+    unpack(mesh_n, mol, owners, row_idx * cols_n + col_idx, pieces, early, x_ref, q_ref, pref_ref)
     sub8 = lax.broadcasted_iota(jnp.int32, (8, LANES), 0)
     lane8 = lax.broadcasted_iota(jnp.int32, (8, LANES), 1)
     gap = lane8 - sub8
@@ -243,35 +244,35 @@
         copy.wait()
 
 
-def squares_kernel(count, *refs):
-    for i, piece in enumerate(refs[:-1]):
-        refs[-1][i * count:(i + 1) * count, :] = squares(piece[0:count, :])
+def early_kernel(mesh_n, mol, owners, *refs):
+    me = lax.axis_index("row") * mesh_n[1] + lax.axis_index("col")
+    for piece, masks in zip(refs, owners):
+        place(mesh_n, mol, me, piece, masks, *refs[-2:])
 
 
 def compute(pieces, mesh_n, mol, owners, early, rows, cols):
     n, width = mol * mesh_n[0] * mesh_n[1], pieces[0].shape[1]
     win = -(-(rows + LANES - math.gcd(rows, LANES)) // LANES) * LANES
-    count = len(owners[0]) * mol
-    sums = pl.pallas_call(
-        functools.partial(squares_kernel, count),
-        out_shape=jax.ShapeDtypeStruct((len(early) * count, LANES), F32),
+    held = [jax.ShapeDtypeStruct((n, width), BF16), jax.ShapeDtypeStruct((n, LANES), F32)]
+    first = pl.pallas_call(
+        functools.partial(early_kernel, mesh_n, mol, [owners[i] for i in early]),
+        out_shape=held,
         in_specs=[pl.BlockSpec(memory_space=pltpu.VMEM)] * len(early),
-        out_specs=pl.BlockSpec(memory_space=pltpu.VMEM),
-        cost_estimate=pl.CostEstimate(flops=len(early) * count * 4 * width * LANES, bytes_accessed=4 << 20, transcendentals=0),
+        out_specs=[pl.BlockSpec(memory_space=pltpu.VMEM)] * 2,
+        cost_estimate=pl.CostEstimate(flops=4 * n * width * LANES, bytes_accessed=4 << 20, transcendentals=0),
         compiler_params=pltpu.CompilerParams(vmem_limit_bytes=40 << 20),
     )(*[pieces[i] for i in early])
     return pl.pallas_call(
         functools.partial(kernel, mesh_n, mol, owners, early, rows, cols, win),
-        out_shape=[jax.ShapeDtypeStruct((rows, cols), F32)] * 2,
-        in_specs=[pl.BlockSpec(memory_space=pltpu.VMEM)] * (len(pieces) + 1),
-        out_specs=[pl.BlockSpec(memory_space=pl.ANY)] * 2,
+        out_shape=[jax.ShapeDtypeStruct((rows, cols), F32)] * 2 + held,
+        in_specs=[pl.BlockSpec(memory_space=pltpu.VMEM)] * (len(pieces) + 2),
+        out_specs=[pl.BlockSpec(memory_space=pl.ANY)] * 2 + [pl.BlockSpec(memory_space=pltpu.VMEM)] * 2,
+        input_output_aliases={0: 2, 1: 3},
         scratch_shapes=[
-            pltpu.VMEM((n, width), BF16),
             pltpu.VMEM((mesh_n[0], width), F32),
             pltpu.VMEM((n, n), F32),
             pltpu.VMEM((LANES, n), F32),
             pltpu.VMEM((LANES, n), F32),
-            pltpu.VMEM((n, LANES), F32),
             pltpu.VMEM((12, 8, n), F32),
             pltpu.VMEM((2, 8, n), jnp.int32),
             pltpu.VMEM((LANES, cols // LANES * win), F32),
@@ -280,7 +281,7 @@
             pltpu.SemaphoreType.DMA((cols // LANES, 2)),
         ],
         compiler_params=pltpu.CompilerParams(vmem_limit_bytes=40 << 20),
-    )(sums, *pieces)
+    )(*first, *pieces)[:2]
 
 
 def pack_kernel(mol, embedding_ref, preference_ref, out_ref, e_ref, p_ref, sems):

time: 27.9 us -> 28 us (level)
  no operation moved by 1% of the time
where the time goes in v6:
time: 28 us; the launch traced here: 27.8 us
  starting transfers between devices  9.6 us (34%)
  Pallas kernels  8.91 us (32%)
  waiting for transfers between devices  8.64 us (31%)
  between operations  0.66 us (2%)
    ppermute x10, starting transfers between devices, swap(): lax.ppermute(block, ('row', 'col'), [(i, i ^ mask) for i in range(size)])  9.6 us
    ppermute x10, waiting for transfers between devices, swap(): lax.ppermute(block, ('row', 'col'), [(i, i ^ mask) for i in range(size)])  8.64 us
    pallas_call x1, Pallas kernels, compute(): pl.pallas_call(functools.partial(kernel, mesh_n, mol, owners, early, rows...  7.58 us
    pallas_call x1, Pallas kernels, pack(): pl.pallas_call(functools.partial(pack_kernel, mol), out_shape=pltpu.VMEM(...  0.8 us
  transfers between devices with their start and end apart: 10, of which 6 were waited for; matrix products, arithmetic and copies ran while one was open for 0% of the time, Pallas kernels for 2%

profile of v6, /device:TPU:0, one launch (start us, length us, event | category | flops | bytes accessed | tf_op | source)
XLA Modules:
  0.0 27.8 jit_solution(11002962690061612628)
XLA Ops:
  0.6 0.8 %shard_map.41 = bf16[56,256]{1,0:T(8,128)(2,1)S(1)} custom-call(bf16[48,256]{1,0:T(8,128)(2,1)} %bitcast.2, f32[1,192]{1,0:T(1,128)} %bitcast.3), custom_call_target="tpu_custom_call" | custom-call | tf_op jit(solution)/shard_map/pallas_call | solution.py:308
  1.4 4.6 %collective-permute-start.2 = (bf16[56,256]{1,0:T(8,128)(2,1)S(1)}, bf16[56,256]{1,0:T(8,128)(2,1)S(1)}, u32[]{:S(2)}, u32[]{:S(2)}) collective-permute-start(bf16[56,256]{1,0:T(8,128)(2,1)S(1)} %shard_map.41), channel_id=1, source_target_pairs={{0,25},{1,24},{2,27},{3,26},{4,29},{5,28},{6,31},{7,30},{8,17},{9,... | collective-permute-start | bytes 86024 | tf_op jit(solution)/shard_map/ppermute | solution.py:333
  6.0 0.0 collective-permute-start.1
  6.0 0.9 %collective-permute-start = (bf16[56,256]{1,0:T(8,128)(2,1)S(1)}, bf16[56,256]{1,0:T(8,128)(2,1)S(1)}, u32[]{:S(2)}, u32[]{:S(2)}) collective-permute-start(bf16[56,256]{1,0:T(8,128)(2,1)S(1)} %shard_map.41), channel_id=1, source_target_pairs={{0,9},{1,8},{2,11},{3,10},{4,13},{5,12},{6,15},{7,14},{8,1},{9,0},... | collective-permute-start | bytes 86024 | tf_op jit(solution)/shard_map/ppermute | solution.py:333
  6.9 2.4 %collective-permute-done = bf16[56,256]{1,0:T(8,128)(2,1)S(1)} collective-permute-done((bf16[56,256]{1,0:T(8,128)(2,1)S(1)}, bf16[56,256]{1,0:T(8,128)(2,1)S(1)}, u32[]{:S(2)}, u32[]{:S(2)}) %collective-permute-start) | collective-permute-done | bytes 28704 | tf_op jit(solution)/shard_map/ppermute | solution.py:333
  9.3 1.1 %collective-permute-done.1 = bf16[56,256]{1,0:T(8,128)(2,1)S(1)} collective-permute-done((bf16[56,256]{1,0:T(8,128)(2,1)S(1)}, bf16[56,256]{1,0:T(8,128)(2,1)S(1)}, u32[]{:S(2)}, u32[]{:S(2)}) %collective-permute-start.1) | collective-permute-done | bytes 28704 | tf_op jit(solution)/shard_map/ppermute | solution.py:333
  10.4 0.0 collective-permute-done.2
  10.5 2.6 %collective-permute-start.5 = (bf16[200,256]{1,0:T(8,128)(2,1)S(1)}, bf16[200,256]{1,0:T(8,128)(2,1)S(1)}, u32[]{:S(2)}, u32[]{:S(2)}) collective-permute-start(bf16[200,256]{1,0:T(8,128)(2,1)S(1)} %constant_dynamic-update-slice_fusion.refs_0_.refs_2_), channel_id=1, source_target_pairs={{0,7},{1,6},{2,5},{3,4},{4,3},{5,2},{6,1},{7,0},{8,15},{9,14},{10,... | collective-permute-start | bytes 307208 | tf_op jit(solution)/shard_map/ppermute | solution.py:333
  13.0 0.2 collective-permute-start.4
  13.2 0.6 %collective-permute-start.3 = (bf16[200,256]{1,0:T(8,128)(2,1)S(1)}, bf16[200,256]{1,0:T(8,128)(2,1)S(1)}, u32[]{:S(2)}, u32[]{:S(2)}) collective-permute-start(bf16[200,256]{1,0:T(8,128)(2,1)S(1)} %constant_dynamic-update-slice_fusion.refs_0_.refs_2_), channel_id=1, source_target_pairs={{0,3},{1,2},{2,1},{3,0},{4,7},{5,6},{6,5},{7,4},{8,11},{9,10},{10,... | collective-permute-start | bytes 307208 | tf_op jit(solution)/shard_map/ppermute | solution.py:333
  13.8 0.1 collective-permute-start.6
  13.9 2.4 %collective-permute-done.5.refs_3_.refs_5_ = bf16[200,256]{1,0:T(8,128)(2,1)S(1)} collective-permute-done((bf16[200,256]{1,0:T(8,128)(2,1)S(1)}, bf16[200,256]{1,0:T(8,128)(2,1)S(1)}, u32[]{:S(2)}, u32[]{:S(2)}) %collective-permute-start.5) | collective-permute-done | bytes 102432 | tf_op jit(solution)/shard_map/ppermute | solution.py:333
  16.3 0.2 collective-permute-start.7
  16.5 2.3 %collective-permute-done.4.refs_2_.refs_4_ = bf16[200,256]{1,0:T(8,128)(2,1)S(1)} collective-permute-done((bf16[200,256]{1,0:T(8,128)(2,1)S(1)}, bf16[200,256]{1,0:T(8,128)(2,1)S(1)}, u32[]{:S(2)}, u32[]{:S(2)}) %collective-permute-start.4) | collective-permute-done | bytes 102432 | tf_op jit(solution)/shard_map/ppermute | solution.py:333
  18.8 0.1 collective-permute-start.9
  18.9 0.0 collective-permute-done.3.refs_1_.refs_3_
  18.9 0.4 %collective-permute-start.8 = (bf16[200,256]{1,0:T(8,128)(2,1)S(1)}, bf16[200,256]{1,0:T(8,128)(2,1)S(1)}, u32[]{:S(2)}, u32[]{:S(2)}) collective-permute-start(bf16[200,256]{1,0:T(8,128)(2,1)S(1)} %collective-permute-done.3.refs_1_.refs_3_), channel_id=1, source_target_pairs={{0,1},{1,0},{2,3},{3,2},{4,5},{5,4},{6,7},{7,6},{8,9},{9,8},{10,11... | collective-permute-start | bytes 307208 | tf_op jit(solution)/shard_map/ppermute | solution.py:333
  19.3 0.0 collective-permute-done.6.refs_4_.refs_6_
  19.3 0.0 collective-permute-done.7.refs_5_.refs_9_
  19.3 0.5 %shard_map.42 = (bf16[1536,256]{1,0:T(8,128)(2,1)S(1)}, f32[1536,128]{1,0:T(8,128)S(1)}) custom-call(bf16[200,256]{1,0:T(8,128)(2,1)S(1)} %constant_dynamic-update-slice_fusion.refs_0_.refs_2_, bf16[200,256]{1,0:T(8,128)(2,1)S(1)} %collective-permute-done.3.refs_1_.refs_3_, bf16[200,256]{1,0:T(8,128)(2,1)S(1)} %collective-permute-done.4.refs_2_.refs_4_, ...), custom_call_target="tpu_custom_call" | custom-call | flops 201326592 | bytes 4194304 | tf_op jit(solution)/shard_map/pallas_call | solution.py:257
  19.9 0.2 collective-permute-done.9.refs_8_
  20.1 0.2 collective-permute-done.8.refs_7_
  20.3 7.6 %shard_map.43 = (f32[192,384]{1,0:T(8,128)}, f32[192,384]{1,0:T(8,128)}, bf16[1536,256]{1,0:T(8,128)(2,1)S(1)}, f32[1536,128]{1,0:T(8,128)S(1)}) custom-call(bf16[1536,256]{1,0:T(8,128)(2,1)S(1)} %get-tuple-element.6.refs_0_, f32[1536,128]{1,0:T(8,128)S(1)} %get-tuple-element.7.refs_1_, ...), custom_call_target="tpu_custom_call", output_to_operand_aliasing={{2}: (0, {}), {3}: (1, {})} | custom-call | tf_op jit(solution)/shard_map/pallas_call | solution.py:265
  (5 shorter events, 0.0 us)
Async XLA Ops:
  1.4 9.0 %collective-permute-start.2 = (bf16[56,256]{1,0:T(8,128)(2,1)S(1)}, bf16[56,256]{1,0:T(8,128)(2,1)S(1)}, u32[]{:S(2)}, u32[]{:S(2)}) collective-permute-start(bf16[56,256]{1,0:T(8,128)(2,1)S(1)} %shard_map.41), channel_id=1, source_target_pairs={{0,25},{1,24},{2,27},{3,26},{4,29},{5,28},{6,31},{7,30},{8,17},{9,... | collective-permute-start | bytes 86024 | tf_op jit(solution)/shard_map/ppermute | solution.py:333
  6.0 4.5 %collective-permute-start.1 = (bf16[56,256]{1,0:T(8,128)(2,1)S(1)}, bf16[56,256]{1,0:T(8,128)(2,1)S(1)}, u32[]{:S(2)}, u32[]{:S(2)}) collective-permute-start(bf16[56,256]{1,0:T(8,128)(2,1)S(1)} %shard_map.41), channel_id=1, source_target_pairs={{0,17},{1,16},{2,19},{3,18},{4,21},{5,20},{6,23},{7,22},{8,25},{9,... | collective-permute-start | bytes 86024 | tf_op jit(solution)/shard_map/ppermute | solution.py:333
  6.0 3.3 %collective-permute-start = (bf16[56,256]{1,0:T(8,128)(2,1)S(1)}, bf16[56,256]{1,0:T(8,128)(2,1)S(1)}, u32[]{:S(2)}, u32[]{:S(2)}) collective-permute-start(bf16[56,256]{1,0:T(8,128)(2,1)S(1)} %shard_map.41), channel_id=1, source_target_pairs={{0,9},{1,8},{2,11},{3,10},{4,13},{5,12},{6,15},{7,14},{8,1},{9,0},... | collective-permute-start | bytes 86024 | tf_op jit(solution)/shard_map/ppermute | solution.py:333
  10.5 5.8 %collective-permute-start.5 = (bf16[200,256]{1,0:T(8,128)(2,1)S(1)}, bf16[200,256]{1,0:T(8,128)(2,1)S(1)}, u32[]{:S(2)}, u32[]{:S(2)}) collective-permute-start(bf16[200,256]{1,0:T(8,128)(2,1)S(1)} %constant_dynamic-update-slice_fusion.refs_0_.refs_2_), channel_id=1, source_target_pairs={{0,7},{1,6},{2,5},{3,4},{4,3},{5,2},{6,1},{7,0},{8,15},{9,14},{10,... | collective-permute-start | bytes 307208 | tf_op jit(solution)/shard_map/ppermute | solution.py:333
  13.0 5.8 %collective-permute-start.4 = (bf16[200,256]{1,0:T(8,128)(2,1)S(1)}, bf16[200,256]{1,0:T(8,128)(2,1)S(1)}, u32[]{:S(2)}, u32[]{:S(2)}) collective-permute-start(bf16[200,256]{1,0:T(8,128)(2,1)S(1)} %constant_dynamic-update-slice_fusion.refs_0_.refs_2_), channel_id=1, source_target_pairs={{0,5},{1,4},{2,7},{3,6},{4,1},{5,0},{6,3},{7,2},{8,13},{9,12},{10,... | collective-permute-start | bytes 307208 | tf_op jit(solution)/shard_map/ppermute | solution.py:333
  13.2 5.7 %collective-permute-start.3 = (bf16[200,256]{1,0:T(8,128)(2,1)S(1)}, bf16[200,256]{1,0:T(8,128)(2,1)S(1)}, u32[]{:S(2)}, u32[]{:S(2)}) collective-permute-start(bf16[200,256]{1,0:T(8,128)(2,1)S(1)} %constant_dynamic-update-slice_fusion.refs_0_.refs_2_), channel_id=1, source_target_pairs={{0,3},{1,2},{2,1},{3,0},{4,7},{5,6},{6,5},{7,4},{8,11},{9,10},{10,... | collective-permute-start | bytes 307208 | tf_op jit(solution)/shard_map/ppermute | solution.py:333
  13.8 5.5 %collective-permute-start.6 = (bf16[200,256]{1,0:T(8,128)(2,1)S(1)}, bf16[200,256]{1,0:T(8,128)(2,1)S(1)}, u32[]{:S(2)}, u32[]{:S(2)}) collective-permute-start(bf16[200,256]{1,0:T(8,128)(2,1)S(1)} %constant_dynamic-update-slice_fusion.refs_0_.refs_2_), channel_id=1, source_target_pairs={{0,1},{1,0},{2,3},{3,2},{4,5},{5,4},{6,7},{7,6},{8,9},{9,8},{10,11... | collective-permute-start | bytes 307208 | tf_op jit(solution)/shard_map/ppermute | solution.py:333
  16.3 3.0 %collective-permute-start.7 = (bf16[200,256]{1,0:T(8,128)(2,1)S(1)}, bf16[200,256]{1,0:T(8,128)(2,1)S(1)}, u32[]{:S(2)}, u32[]{:S(2)}) collective-permute-start(bf16[200,256]{1,0:T(8,128)(2,1)S(1)} %collective-permute-done.5.refs_3_.refs_5_), channel_id=1, source_target_pairs={{0,1},{1,0},{2,3},{3,2},{4,5},{5,4},{6,7},{7,6},{8,9},{9,8},{10,11... | collective-permute-start | bytes 307208 | tf_op jit(solution)/shard_map/ppermute | solution.py:333
  18.8 1.3 %collective-permute-start.9 = (bf16[200,256]{1,0:T(8,128)(2,1)S(1)}, bf16[200,256]{1,0:T(8,128)(2,1)S(1)}, u32[]{:S(2)}, u32[]{:S(2)}) collective-permute-start(bf16[200,256]{1,0:T(8,128)(2,1)S(1)} %collective-permute-done.4.refs_2_.refs_4_), channel_id=1, source_target_pairs={{0,1},{1,0},{2,3},{3,2},{4,5},{5,4},{6,7},{7,6},{8,9},{9,8},{10,11... | collective-permute-start | bytes 307208 | tf_op jit(solution)/shard_map/ppermute | solution.py:333
  18.9 1.3 %collective-permute-start.8 = (bf16[200,256]{1,0:T(8,128)(2,1)S(1)}, bf16[200,256]{1,0:T(8,128)(2,1)S(1)}, u32[]{:S(2)}, u32[]{:S(2)}) collective-permute-start(bf16[200,256]{1,0:T(8,128)(2,1)S(1)} %collective-permute-done.3.refs_1_.refs_3_), channel_id=1, source_target_pairs={{0,1},{1,0},{2,3},{3,2},{4,5},{5,4},{6,7},{7,6},{8,9},{9,8},{10,11... | collective-permute-start | bytes 307208 | tf_op jit(solution)/shard_map/ppermute | solution.py:333
